TPU v7x, 512 devices: a whole 4x4x16 slice. The times are simulated.
512 devices in a mesh: prow: 16 (over x, y_lo, core), pcol: 32 (over y_hi, z).
Axes of the slice: x: 4, y: 4 (y_hi: 2, y_lo: 2; y = y_hi * 2 + y_lo), z: 16, core: 2. Of those that a mesh axis runs over, the one named last changes fastest.
Arguments:
- mantissa: bfloat16 [20480, 1024], P(('pcol', 'prow')), may hold values from -0.5 to 0.5
- exponent: int32 [20480, 8], P(('pcol', 'prow')), may hold values from -2 to 2
- occ_level: int32 [1024], replicated, may hold values from -300 to -21
- virt_level: int32 [1024], replicated, may hold values from 50 to 399
Outputs:
- response: float32 [20480, 20480], P('prow', 'pcol')
All inputs are finite; a program needn't handle non-finite values.
Results may differ from a plain program's by a relative error of at most 0.00064.
Values may be sent and summed in bfloat16 or wider, within the bound.
No kernel may reach another device: no remote copies, remote signals or barrier semaphores. Data moves between devices by JAX's collectives and lax.ppermute only.
A program may use at most 64 MiB of HBM per device.

v0:
```python
import jax
import jax.numpy as jnp
from jax import lax
from jax.sharding import PartitionSpec as P


def from_root(block, axis, holder):
    block = jnp.where(lax.axis_index(axis) == holder, block, jnp.zeros_like(block))
    return lax.psum(block, axis)


def dequantize(mantissa, exponent):
    block_scale = jnp.exp2(exponent.astype(jnp.float32))
    full_scale = jnp.repeat(block_scale, 128, axis=1)
    return (mantissa.astype(jnp.float32) * full_scale).astype(jnp.bfloat16)


def pair_weights(occ_level, virt_level):
    energy_gap = 0.01 * (virt_level - occ_level).astype(jnp.float32)
    return -4.0 * energy_gap / (energy_gap * energy_gap + 1.0)


def per_device(mantissa, exponent, occ_level, virt_level):
    own_block = dequantize(mantissa, exponent)
    row_devices = lax.axis_size("prow")
    col_devices = lax.axis_size("pcol")
    fold_ratio = col_devices // row_devices
    q_rows = lax.all_gather(own_block, "prow", axis=0, tiled=True)
    first_root = lax.axis_index("prow") * fold_ratio
    pieces = [from_root(q_rows, "pcol", first_root + step) for step in range(fold_ratio)]
    p_rows = jnp.concatenate(pieces, axis=0)
    weights = pair_weights(occ_level, virt_level)
    scaled = (q_rows.astype(jnp.float32) * weights[None, :]).astype(jnp.bfloat16)
    return lax.dot_general(
        p_rows, scaled, (((1,), (1,)), ((), ())), preferred_element_type=jnp.float32
    )


def solution(mesh):
    return jax.shard_map(
        per_device,
        mesh=mesh,
        in_specs=(P(("pcol", "prow"), None), P(("pcol", "prow"), None), P(), P()),
        out_specs=P("prow", "pcol"),
        check_vma=False,
    )
```

profile of v0, /device:TPU:2, one launch (start us, length us, event | category | flops | bytes accessed | tf_op | source)
XLA Modules:
  0.0 380.1 jit_solution(7408671703899313982)
XLA Ops:
  6.5 0.0 all-gather.2.cloned.1.call-start
  6.5 0.7 multiply_exponential_fusion
  7.2 0.1 copy.5
  7.3 0.1 broadcast_in_dim.4
  7.4 1.6 fusion.5
  9.0 0.0 all-gather.2.cloned.1.call-update
  9.0 0.0 all-reduce.3.cloned.1.call-start
  9.1 45.1 %all-gather.2.cloned.1.call-done = bf16[640,1024]{1,0:T(8,128)(2,1)} async-done(((bf16[40,1024]{1,0:T(8,128)(2,1)}), bf16[640,1024]{1,0:T(8,128)(2,1)}) %all-gather.2.cloned.1.call-update) | async-done | bytes 1310736 | tf_op jit(solution)/shard_map/all_gather | solution.py:28
  54.2 3.0 broadcast_select_fusion.1
  57.2 0.0 copy-start.1
  57.2 0.0 copy-start.2
  57.2 0.0 copy-start
  57.2 0.0 all-reduce.3.cloned.1.call-update
  57.2 0.7 copy-done.1
  57.8 0.0 copy-done.2
  57.9 309.7 %all-reduce.3.cloned.1.call-done = (bf16[640,1024]{1,0:T(8,128)(2,1)}, bf16[640,1024]{1,0:T(8,128)(2,1)}) async-done(((bf16[640,1024]{1,0:T(8,128)(2,1)}, bf16[640,1024]{1,0:T(8,128)(2,1)}), (bf16[640,1024]{1,0:T(8,128)(2,1)}, bf16[640,1024]{1,0:T(8,128)(2,1)})) %all-reduce.3.cloned.1.call-update) | async-done | bytes 2621456 | tf_op jit(solution)/shard_map/psum | solution.py:9
  367.6 0.0 copy-done
  367.6 5.7 %fusion = f32[1280,640]{1,0:T(8,128)} fusion(bf16[640,1024]{1,0:T(8,128)(2,1)} %get-tuple-element.5, bf16[640,1024]{1,0:T(8,128)(2,1)} %get-tuple-element.6, bf16[640,1024]{1,0:T(8,128)(2,1)S(1)} %copy-done, f32[1024]{0:T(1024)S(1)} %add_divide_fusion), kind=kOutput, calls=%fused_computation | convolution fusion | flops 1684930560 | bytes 7213056 | tf_op jit(solution)/shard_map/dot_general | solution.py:34
  (1 shorter events, 0.0 us)
Async XLA Ops:
  6.5 47.7 %all-gather.2.cloned.1.call-start = ((), (), s32[]{:S(2)}) async-start(), calls=%async_computation | async-start | bytes 1392640 | tf_op jit(solution)/shard_map/all_gather | solution.py:28
  9.0 358.5 %all-reduce.3.cloned.1.call-start = ((), (), s32[]{:S(2)}) async-start(), calls=%async_computation.1 | async-start | bytes 5242880 | tf_op jit(solution)/shard_map/psum | solution.py:9
  57.2 0.7 copy-start.1
  57.2 0.7 copy-start.2
  57.2 310.4 %copy-start = (bf16[640,1024]{1,0:T(8,128)(2,1)S(1)}, bf16[640,1024]{1,0:T(8,128)(2,1)}, u32[]{:S(2)}) copy-start(bf16[640,1024]{1,0:T(8,128)(2,1)} %all-gather.2.cloned.1.call-done) | copy-start | bytes 3932164
Sparse Core Ops, SparseCore 0:
  9.5 44.6 all-gather.1
  57.3 310.2 all-reduce.2
where the time goes:
time: 380 us
  waiting for transfers between devices  355 us (93%)
  between operations  13.4 us (4%)
  matrix products  5.66 us (1%)
  other arithmetic  5.22 us (1%)
    psum x1, waiting for transfers between devices, from_root(): return lax.psum(block, axis)  310 us
    all_gather x1, waiting for transfers between devices, per_device(): q_rows = lax.all_gather(own_block, 'prow', axis=0, tiled=True)  45.1 us
  transfers between devices with their start and end apart: 2, of which 2 were waited for; matrix products, arithmetic and copies ran while one was open for 0% of the time, Pallas kernels for 0%

commit v1 on v0

v1 whole, which is shorter than its diff:
```python
import jax
import jax.numpy as jnp
from jax import lax
from jax.experimental import pallas as pl
from jax.experimental.pallas import tpu as pltpu
from jax.sharding import PartitionSpec as P

NX, NY, NZ = 4, 4, 16
ROWS = 160
CHUNKS = 8
DEPTH = 1024
COLS = 640
JOINT = ("prow", "pcol")
LIMIT = 32 * 1024 * 1024


def split(index):
    row, col = divmod(index, 2 * NZ)
    return row >> 2, (col // NZ) * 2 + ((row >> 1) & 1), col % NZ, row & 1


def join(x, y, z, core):
    x, y, z = x % NX, y % NY, z % NZ
    return (x * 4 + (y & 1) * 2 + core) * 2 * NZ + (y >> 1) * NZ + z


def shift(dx=0, dy=0, dz=0):
    pairs = []
    for source in range(2 * NX * NY * NZ):
        x, y, z, core = split(source)
        pairs.append((source, join(x + dx, y + dy, z + dz, core)))
    return pairs


def spread():
    pairs = []
    for source in range(2 * NX * NY * NZ):
        x, y, z, core = split(source)
        col = (y >> 1) * NZ + z
        row, half = col // 2, col % 2
        chunk = 4 * half + x
        y_hi = (y & 1) ^ ((row >> 1) & 1)
        z_to = (chunk - 4 * y_hi + 2 * row) % 8 + 8 * core
        pairs.append((source, row * 2 * NZ + y_hi * NZ + z_to))
    return pairs


def send(block, pairs):
    return lax.ppermute(block, JOINT, pairs)


def dequantize_body(mantissa, exponent, out):
    scale = jnp.exp2(exponent[...].astype(jnp.float32))
    for k in range(DEPTH // 128):
        span = slice(128 * k, 128 * (k + 1))
        out[:, span] = (mantissa[:, span].astype(jnp.float32) * scale[:, k : k + 1]).astype(jnp.bfloat16)


def dequantize(mantissa, exponent):
    return pl.pallas_call(
        dequantize_body,
        out_shape=jax.ShapeDtypeStruct(mantissa.shape, jnp.bfloat16),
        compiler_params=pltpu.CompilerParams(vmem_limit_bytes=LIMIT),
    )(mantissa, exponent)


def scale_body(place, weights, own, before, after, across, out):
    for step, block in ((0, own), (3, before), (1, after), (2, across)):
        start = pl.multiple_of(lax.rem(place[0] + step, 4) * ROWS, ROWS)
        out[pl.ds(start, ROWS), :] = (block[...].astype(jnp.float32) * weights[...]).astype(jnp.bfloat16)


def scale(place, weights, own, before, after, across):
    whole = pl.BlockSpec(memory_space=pltpu.VMEM)
    return pl.pallas_call(
        scale_body,
        out_shape=jax.ShapeDtypeStruct((COLS, DEPTH), jnp.bfloat16),
        in_specs=[pl.BlockSpec(memory_space=pltpu.SMEM)] + [whole] * 5,
        out_specs=whole,
        compiler_params=pltpu.CompilerParams(vmem_limit_bytes=LIMIT),
        cost_estimate=pl.CostEstimate(flops=COLS * DEPTH, bytes_accessed=4 * COLS * DEPTH, transcendentals=0),
    )(place, weights, own, before, after, across)


def multiply_body(colors, rows, columns, *rest):
    out = rest[-1]
    out[0] = lax.dot_general(
        rows[...], columns[...], (((1,), (1,)), ((), ())), preferred_element_type=jnp.float32
    )


def multiply(colors, rows, columns, response):
    count = rows.shape[0] // ROWS
    in_specs = [
        pl.BlockSpec((ROWS, DEPTH), lambda i, colors: (i, 0)),
        pl.BlockSpec((COLS, DEPTH), lambda i, colors: (0, 0)),
    ]
    args = [colors, rows, columns]
    aliases = {}
    if response is not None:
        in_specs.append(pl.BlockSpec(memory_space=pl.ANY))
        args.append(response)
        aliases = {3: 0}
    return pl.pallas_call(
        multiply_body,
        out_shape=jax.ShapeDtypeStruct((CHUNKS, ROWS, COLS), jnp.float32),
        grid_spec=pltpu.PrefetchScalarGridSpec(
            num_scalar_prefetch=1,
            grid=(count,),
            in_specs=in_specs,
            out_specs=pl.BlockSpec((1, ROWS, COLS), lambda i, colors: (colors[i], 0, 0)),
        ),
        input_output_aliases=aliases,
        compiler_params=pltpu.CompilerParams(vmem_limit_bytes=LIMIT),
        cost_estimate=pl.CostEstimate(
            flops=2 * count * ROWS * COLS * DEPTH,
            bytes_accessed=count * ROWS * (2 * DEPTH + 4 * COLS) + 2 * COLS * DEPTH,
            transcendentals=0,
        ),
    )(*args)


def pair_weights(occ_level, virt_level):
    energy_gap = 0.01 * (virt_level - occ_level).astype(jnp.float32)
    return -4.0 * energy_gap / (energy_gap * energy_gap + 1.0)


def per_device(mantissa, exponent, occ_level, virt_level):
    row, col = lax.axis_index("prow"), lax.axis_index("pcol")
    color = (col % NZ + 4 * (col // NZ) - 2 * row) % CHUNKS

    own = dequantize(mantissa, exponent)
    same_x = [[4 * x + i for i in range(4)] for x in range(NX)]
    group = lax.all_gather(own, "prow", axis=0, tiled=True, axis_index_groups=same_x)

    placed = send(group, spread())
    before = send(group, shift(dx=1))
    after = send(group, shift(dx=-1))
    across = send(group, shift(dx=2))

    down = send(placed, shift(dz=1))
    up = send(placed, shift(dz=-1))
    near = jnp.concatenate([placed, down, up], axis=0)
    far = send(near, shift(dy=2))
    down_two = send(down, shift(dz=1))
    up_two = send(up, shift(dz=-1))

    weights = pair_weights(occ_level, virt_level)[None, :]
    columns = scale((row // 4)[None], weights, group, before, after, across)

    def colors(*steps):
        return (color + jnp.array(steps, jnp.int32)) % CHUNKS

    response = multiply(colors(0, 7, 1), near, columns, None)
    response = multiply(colors(6), down_two, columns, response)
    response = multiply(colors(2), up_two, columns, response)
    response = multiply(colors(4, 3, 5), far, columns, response)
    return response.reshape(CHUNKS * ROWS, COLS)


def solution(mesh):
    return jax.shard_map(
        per_device,
        mesh=mesh,
        in_specs=(P(("pcol", "prow"), None), P(("pcol", "prow"), None), P(), P()),
        out_specs=P("prow", "pcol"),
        check_vma=False,
    )
```

time: 380 us -> 95.8 us (0.25)
  the two profiles are of different devices: /device:TPU:2 before, /device:TPU:186 now
where the time goes in v1:
time: 95.8 us; the launch traced here: 95.3 us
  waiting for transfers between devices  39.2 us (41%)
  starting transfers between devices  34 us (35%)
  Pallas kernels  10.5 us (11%)
  blocking collectives  5.97 us (6%)
  local copies, waits for them, and re-layouts  3.41 us (4%)
  other arithmetic  2.05 us (2%)
    ppermute x9, waiting for transfers between devices, send(): return lax.ppermute(block, JOINT, pairs)  39.2 us
    ppermute x9, starting transfers between devices, send(): return lax.ppermute(block, JOINT, pairs)  34 us
    pallas_call x4, Pallas kernels, multiply(): pl.pallas_call(multiply_body, out_shape=jax.ShapeDtypeStruct((CHUNKS, ROW...  9.05 us
    all_gather x1, blocking collectives, per_device(): lax.all_gather(own, 'prow', axis=0, tiled=True, axis_index_groups=same_x)  5.97 us
    unnamed x7, local copies, waits for them, and re-layouts  3.39 us
  transfers between devices with their start and end apart: 9, of which 4 were waited for; matrix products, arithmetic and copies ran while one was open for 3% of the time, Pallas kernels for 7%

profile of v1, /device:TPU:186, one launch (start us, length us, event | category | flops | bytes accessed | tf_op | source)
XLA Modules:
  0.0 95.3 jit_solution(7644722678281700038)
XLA Ops:
  0.0 0.8 copy.12.exponent
  0.8 0.9 copy-done
  1.7 0.1 shard_map.82
  1.8 6.0 %all_gather.3.own = bf16[160,1024]{1,0:T(8,128)(2,1)S(1)} all-gather(bf16[40,1024]{1,0:T(8,128)(2,1)S(1)} %shard_map.82), channel_id=1, replica_groups={{0,32,64,96},{128,160,192,224},{256,288,320,352},{384,416,448,480},{1,3..., dimensions={0}, use_global_device_ids=true | all-gather | bytes 409600 | tf_op jit(solution)/shard_map/all_gather | solution.py:134
  7.7 2.2 %collective-permute-start = (bf16[160,1024]{1,0:T(8,128)(2,1)S(1)}, bf16[160,1024]{1,0:T(8,128)(2,1)S(1)}, u32[]{:S(2)}, u32[]{:S(2)}) collective-permute-start(bf16[160,1024]{1,0:T(8,128)(2,1)S(1)} %all_gather.3.own), channel_id=1, source_target_pairs={{0,0},{1,4},{2,34},{3,38},{4,80},{5,84},{6,114},{7,118},{8,128},{9... | collective-permute-start | bytes 983048 | tf_op jit(solution)/shard_map/ppermute | solution.py:49
  10.0 24.2 %collective-permute-done = bf16[160,1024]{1,0:T(8,128)(2,1)S(1)} collective-permute-done((bf16[160,1024]{1,0:T(8,128)(2,1)S(1)}, bf16[160,1024]{1,0:T(8,128)(2,1)S(1)}, u32[]{:S(2)}, u32[]{:S(2)}) %collective-permute-start) | collective-permute-done | bytes 327712 | tf_op jit(solution)/shard_map/ppermute | solution.py:49
  34.2 9.4 %collective-permute-start.1 = (bf16[160,1024]{1,0:T(8,128)(2,1)S(1)}, bf16[160,1024]{1,0:T(8,128)(2,1)}, u32[]{:S(2)}, u32[]{:S(2)}) collective-permute-start(bf16[160,1024]{1,0:T(8,128)(2,1)S(1)} %collective-permute-done), channel_id=1, source_target_pairs={{0,1},{1,2},{2,3},{3,4},{4,5},{5,6},{6,7},{7,8},{8,9},{9,10},{10,1... | collective-permute-start | bytes 983048 | tf_op jit(solution)/shard_map/ppermute | solution.py:49
  43.6 1.9 %collective-permute-start.2 = (bf16[160,1024]{1,0:T(8,128)(2,1)S(1)}, bf16[160,1024]{1,0:T(8,128)(2,1)S(1)}, u32[]{:S(2)}, u32[]{:S(2)}) collective-permute-start(bf16[160,1024]{1,0:T(8,128)(2,1)S(1)} %collective-permute-done), channel_id=1, source_target_pairs={{0,15},{1,0},{2,1},{3,2},{4,3},{5,4},{6,5},{7,6},{8,7},{9,8},{10,9... | collective-permute-start | bytes 983048 | tf_op jit(solution)/shard_map/ppermute | solution.py:49
  45.6 5.9 %collective-permute-done.1 = bf16[160,1024]{1,0:T(8,128)(2,1)} collective-permute-done((bf16[160,1024]{1,0:T(8,128)(2,1)S(1)}, bf16[160,1024]{1,0:T(8,128)(2,1)}, u32[]{:S(2)}, u32[]{:S(2)}) %collective-permute-start.1) | collective-permute-done | bytes 327712 | tf_op jit(solution)/shard_map/ppermute | solution.py:49
  51.4 1.0 %constant_dynamic-update-slice_fusion.1 = bf16[480,1024]{1,0:T(8,128)(2,1)S(1)} fusion(bf16[480,1024]{1,0:T(8,128)(2,1)S(1)} %constant_dynamic-update-slice_fusion.2, bf16[160,1024]{1,0:T(8,128)(2,1)} %collective-permute-done.1), kind=kLoop, calls=%fused_computation.1 | loop fusion | bytes 655360
  52.4 3.6 %collective-permute-done.2 = bf16[160,1024]{1,0:T(8,128)(2,1)S(1)} collective-permute-done((bf16[160,1024]{1,0:T(8,128)(2,1)S(1)}, bf16[160,1024]{1,0:T(8,128)(2,1)S(1)}, u32[]{:S(2)}, u32[]{:S(2)}) %collective-permute-start.2) | collective-permute-done | bytes 327712 | tf_op jit(solution)/shard_map/ppermute | solution.py:49
  56.1 0.7 copy-done.1
  56.8 2.5 %collective-permute-start.3 = (bf16[480,1024]{1,0:T(8,128)(2,1)S(1)}, bf16[480,1024]{1,0:T(8,128)(2,1)S(1)}, u32[]{:S(2)}, u32[]{:S(2)}) collective-permute-start(bf16[480,1024]{1,0:T(8,128)(2,1)S(1)} %constant_dynamic-update-slice_fusion.rows), channel_id=1, source_target_pairs={{0,16},{1,17},{2,18},{3,19},{4,20},{5,21},{6,22},{7,23},{8,24},{9,... | collective-permute-start | bytes 2949128 | tf_op jit(solution)/shard_map/ppermute | solution.py:49
  59.3 1.9 %collective-permute-start.4 = (bf16[160,1024]{1,0:T(8,128)(2,1)S(1)}, bf16[160,1024]{1,0:T(8,128)(2,1)S(1)}, u32[]{:S(2)}, u32[]{:S(2)}) collective-permute-start(bf16[160,1024]{1,0:T(8,128)(2,1)S(1)} %all_gather.3.own), channel_id=1, source_target_pairs={{0,128},{1,129},{2,130},{3,131},{4,132},{5,133},{6,134},{7,135},{8... | collective-permute-start | bytes 983048 | tf_op jit(solution)/shard_map/ppermute | solution.py:49
  61.2 3.9 %collective-permute-start.5 = (bf16[160,1024]{1,0:T(8,128)(2,1)S(1)}, bf16[160,1024]{1,0:T(8,128)(2,1)}, u32[]{:S(2)}, u32[]{:S(2)}) collective-permute-start(bf16[160,1024]{1,0:T(8,128)(2,1)S(1)} %all_gather.3.own), channel_id=1, source_target_pairs={{0,384},{1,385},{2,386},{3,387},{4,388},{5,389},{6,390},{7,391},{8... | collective-permute-start | bytes 983048 | tf_op jit(solution)/shard_map/ppermute | solution.py:49
  65.1 6.4 %collective-permute-start.6 = (bf16[160,1024]{1,0:T(8,128)(2,1)S(1)}, bf16[160,1024]{1,0:T(8,128)(2,1)}, u32[]{:S(2)}, u32[]{:S(2)}) collective-permute-start(bf16[160,1024]{1,0:T(8,128)(2,1)S(1)} %all_gather.3.own), channel_id=1, source_target_pairs={{0,256},{1,257},{2,258},{3,259},{4,260},{5,261},{6,262},{7,263},{8... | collective-permute-start | bytes 983048 | tf_op jit(solution)/shard_map/ppermute | solution.py:49
  71.5 0.7 and_select_fusion.colors
  72.2 1.9 %collective-permute-start.8 = (bf16[160,1024]{1,0:T(8,128)(2,1)}, bf16[160,1024]{1,0:T(8,128)(2,1)S(1)}, u32[]{:S(2)}, u32[]{:S(2)}) collective-permute-start(bf16[160,1024]{1,0:T(8,128)(2,1)} %collective-permute-done.1), channel_id=1, source_target_pairs={{0,1},{1,2},{2,3},{3,4},{4,5},{5,6},{6,7},{7,8},{8,9},{9,10},{10,1... | collective-permute-start | bytes 983048 | tf_op jit(solution)/shard_map/ppermute | solution.py:49
  74.1 0.0 collective-permute-done.4.before
  74.1 3.9 %collective-permute-start.7 = (bf16[160,1024]{1,0:T(8,128)(2,1)}, bf16[160,1024]{1,0:T(8,128)(2,1)S(1)}, u32[]{:S(2)}, u32[]{:S(2)}) collective-permute-start(bf16[160,1024]{1,0:T(8,128)(2,1)} %copy-done.1), channel_id=1, source_target_pairs={{0,15},{1,0},{2,1},{3,2},{4,3},{5,4},{6,5},{7,6},{8,7},{9,8},{10,9... | collective-permute-start | bytes 983048 | tf_op jit(solution)/shard_map/ppermute | solution.py:49
  78.1 0.7 and_select_fusion.1.colors
  78.7 0.7 add_divide_fusion
  79.5 0.0 collective-permute-done.5.after
  79.5 5.5 %collective-permute-done.6.across = bf16[160,1024]{1,0:T(8,128)(2,1)} collective-permute-done((bf16[160,1024]{1,0:T(8,128)(2,1)S(1)}, bf16[160,1024]{1,0:T(8,128)(2,1)}, u32[]{:S(2)}, u32[]{:S(2)}) %collective-permute-start.6) | collective-permute-done | bytes 327712 | tf_op jit(solution)/shard_map/ppermute | solution.py:49
  84.9 1.3 %shard_map.83.columns = bf16[640,1024]{1,0:T(8,128)(2,1)S(1)} custom-call(s32[1]{0:T(128)} %bitcast.place, f32[1,1024]{1,0:T(1,128)S(1)} %bitcast.5, bf16[160,1024]{1,0:T(8,128)(2,1)S(1)} %all_gather.3.own, bf16[160,1024]{1,0:T(8,128)(2,1)S(1)} %collective-permute-done.4.before, bf16[160,1024]{1,0:T(8,128)(2,1)} %collective-permute-done.5.after, ...), custom_call_target="tpu_custom_call" | custom-call | flops 655360 | bytes 2621440 | tf_op jit(solution)/shard_map/pallas_call | solution.py:75
  86.2 3.2 %shard_map.84.rest_0_ = f32[8,160,640]{2,1,0:T(8,128)} custom-call(s32[3]{0:T(128)S(1)} %and_select_fusion.colors, bf16[480,1024]{1,0:T(8,128)(2,1)S(1)} %constant_dynamic-update-slice_fusion.rows, bf16[640,1024]{1,0:T(8,128)(2,1)S(1)} %shard_map.83.columns), custom_call_target="tpu_custom_call" | custom-call | flops 629145600 | bytes 3522560 | tf_op jit(solution)/shard_map/pallas_call | solution.py:104
  89.4 0.0 collective-permute-done.8.rows
  89.4 1.3 %shard_map.85.rest_0_ = f32[8,160,640]{2,1,0:T(8,128)} custom-call(s32[1]{0:T(128)S(6)} %select_n.44.colors, bf16[160,1024]{1,0:T(8,128)(2,1)S(1)} %collective-permute-done.8.rows, bf16[640,1024]{1,0:T(8,128)(2,1)S(1)} %shard_map.83.columns, f32[8,160,640]{2,1,0:T(8,128)} %shard_map.84.rest_0_), custom_call_target="tpu_custom_call", output_to_operand_aliasing={{}: (3, {})} | custom-call | flops 209715200 | bytes 2048000 | tf_op jit(solution)/shard_map/pallas_call | solution.py:104
  90.7 0.0 collective-permute-done.7.rows
  90.7 1.3 %shard_map.86.rest_0_ = f32[8,160,640]{2,1,0:T(8,128)} custom-call(s32[1]{0:T(128)S(6)} %select_n.43.colors, bf16[160,1024]{1,0:T(8,128)(2,1)S(1)} %collective-permute-done.7.rows, bf16[640,1024]{1,0:T(8,128)(2,1)S(1)} %shard_map.83.columns, f32[8,160,640]{2,1,0:T(8,128)} %shard_map.85.rest_0_), custom_call_target="tpu_custom_call", output_to_operand_aliasing={{}: (3, {})} | custom-call | flops 209715200 | bytes 2048000 | tf_op jit(solution)/shard_map/pallas_call | solution.py:104
  92.1 0.0 collective-permute-done.3.rows
  92.1 3.2 %shard_map.87 = f32[8,160,640]{2,1,0:T(8,128)} custom-call(s32[3]{0:T(128)S(1)} %and_select_fusion.1.colors, bf16[480,1024]{1,0:T(8,128)(2,1)S(1)} %collective-permute-done.3.rows, bf16[640,1024]{1,0:T(8,128)(2,1)S(1)} %shard_map.83.columns, f32[8,160,640]{2,1,0:T(8,128)} %shard_map.86.rest_0_), custom_call_target="tpu_custom_call", output_to_operand_aliasing={{}: (3, {})} | custom-call | flops 629145600 | bytes 3522560 | tf_op jit(solution)/shard_map/pallas_call | solution.py:104
  (4 shorter events, 0.0 us)
Async XLA Ops:
  0.8 0.9 copy-start
  7.7 26.5 %collective-permute-start = (bf16[160,1024]{1,0:T(8,128)(2,1)S(1)}, bf16[160,1024]{1,0:T(8,128)(2,1)S(1)}, u32[]{:S(2)}, u32[]{:S(2)}) collective-permute-start(bf16[160,1024]{1,0:T(8,128)(2,1)S(1)} %all_gather.3.own), channel_id=1, source_target_pairs={{0,0},{1,4},{2,34},{3,38},{4,80},{5,84},{6,114},{7,118},{8,128},{9... | collective-permute-start | bytes 983048 | tf_op jit(solution)/shard_map/ppermute | solution.py:49
  34.2 17.2 %collective-permute-start.1 = (bf16[160,1024]{1,0:T(8,128)(2,1)S(1)}, bf16[160,1024]{1,0:T(8,128)(2,1)}, u32[]{:S(2)}, u32[]{:S(2)}) collective-permute-start(bf16[160,1024]{1,0:T(8,128)(2,1)S(1)} %collective-permute-done), channel_id=1, source_target_pairs={{0,1},{1,2},{2,3},{3,4},{4,5},{5,6},{6,7},{7,8},{8,9},{9,10},{10,1... | collective-permute-start | bytes 983048 | tf_op jit(solution)/shard_map/ppermute | solution.py:49
  43.6 12.4 %collective-permute-start.2 = (bf16[160,1024]{1,0:T(8,128)(2,1)S(1)}, bf16[160,1024]{1,0:T(8,128)(2,1)S(1)}, u32[]{:S(2)}, u32[]{:S(2)}) collective-permute-start(bf16[160,1024]{1,0:T(8,128)(2,1)S(1)} %collective-permute-done), channel_id=1, source_target_pairs={{0,15},{1,0},{2,1},{3,2},{4,3},{5,4},{6,5},{7,6},{8,7},{9,8},{10,9... | collective-permute-start | bytes 983048 | tf_op jit(solution)/shard_map/ppermute | solution.py:49
  56.1 0.7 copy-start.1
  56.8 35.2 %collective-permute-start.3 = (bf16[480,1024]{1,0:T(8,128)(2,1)S(1)}, bf16[480,1024]{1,0:T(8,128)(2,1)S(1)}, u32[]{:S(2)}, u32[]{:S(2)}) collective-permute-start(bf16[480,1024]{1,0:T(8,128)(2,1)S(1)} %constant_dynamic-update-slice_fusion.rows), channel_id=1, source_target_pairs={{0,16},{1,17},{2,18},{3,19},{4,20},{5,21},{6,22},{7,23},{8,24},{9,... | collective-permute-start | bytes 2949128 | tf_op jit(solution)/shard_map/ppermute | solution.py:49
  59.3 14.9 %collective-permute-start.4 = (bf16[160,1024]{1,0:T(8,128)(2,1)S(1)}, bf16[160,1024]{1,0:T(8,128)(2,1)S(1)}, u32[]{:S(2)}, u32[]{:S(2)}) collective-permute-start(bf16[160,1024]{1,0:T(8,128)(2,1)S(1)} %all_gather.3.own), channel_id=1, source_target_pairs={{0,128},{1,129},{2,130},{3,131},{4,132},{5,133},{6,134},{7,135},{8... | collective-permute-start | bytes 983048 | tf_op jit(solution)/shard_map/ppermute | solution.py:49
  61.2 18.2 %collective-permute-start.5 = (bf16[160,1024]{1,0:T(8,128)(2,1)S(1)}, bf16[160,1024]{1,0:T(8,128)(2,1)}, u32[]{:S(2)}, u32[]{:S(2)}) collective-permute-start(bf16[160,1024]{1,0:T(8,128)(2,1)S(1)} %all_gather.3.own), channel_id=1, source_target_pairs={{0,384},{1,385},{2,386},{3,387},{4,388},{5,389},{6,390},{7,391},{8... | collective-permute-start | bytes 983048 | tf_op jit(solution)/shard_map/ppermute | solution.py:49
  65.1 19.8 %collective-permute-start.6 = (bf16[160,1024]{1,0:T(8,128)(2,1)S(1)}, bf16[160,1024]{1,0:T(8,128)(2,1)}, u32[]{:S(2)}, u32[]{:S(2)}) collective-permute-start(bf16[160,1024]{1,0:T(8,128)(2,1)S(1)} %all_gather.3.own), channel_id=1, source_target_pairs={{0,256},{1,257},{2,258},{3,259},{4,260},{5,261},{6,262},{7,263},{8... | collective-permute-start | bytes 983048 | tf_op jit(solution)/shard_map/ppermute | solution.py:49
  72.2 17.2 %collective-permute-start.8 = (bf16[160,1024]{1,0:T(8,128)(2,1)}, bf16[160,1024]{1,0:T(8,128)(2,1)S(1)}, u32[]{:S(2)}, u32[]{:S(2)}) collective-permute-start(bf16[160,1024]{1,0:T(8,128)(2,1)} %collective-permute-done.1), channel_id=1, source_target_pairs={{0,1},{1,2},{2,3},{3,4},{4,5},{5,6},{6,7},{7,8},{8,9},{9,10},{10,1... | collective-permute-start | bytes 983048 | tf_op jit(solution)/shard_map/ppermute | solution.py:49
  74.1 16.6 %collective-permute-start.7 = (bf16[160,1024]{1,0:T(8,128)(2,1)}, bf16[160,1024]{1,0:T(8,128)(2,1)S(1)}, u32[]{:S(2)}, u32[]{:S(2)}) collective-permute-start(bf16[160,1024]{1,0:T(8,128)(2,1)} %copy-done.1), channel_id=1, source_target_pairs={{0,15},{1,0},{2,1},{3,2},{4,3},{5,4},{6,5},{7,6},{8,7},{9,8},{10,9... | collective-permute-start | bytes 983048 | tf_op jit(solution)/shard_map/ppermute | solution.py:49

commit v2 on v1

v2 whole, which is shorter than its diff:
```python
import jax
import jax.numpy as jnp
import numpy as np
from jax import lax
from jax.experimental import pallas as pl
from jax.experimental.pallas import tpu as pltpu
from jax.sharding import PartitionSpec as P

NX, NY, NZ = 4, 4, 16
ROWS = 160
CHUNKS = 8
DEPTH = 1024
COLS = 640
JOINT = ("prow", "pcol")
LIMIT = 32 * 1024 * 1024

PLACES = (
    (9, 1, 21, 29, 2, 10, 22, 30, 14, 6, 26, 18, 5, 13, 25, 17, 12, 4, 24, 16, 0, 8, 20, 28, 7, 15, 19, 27, 3, 11, 31, 23),
    (8, 0, 28, 20, 4, 12, 24, 16, 11, 3, 31, 23, 7, 15, 27, 19, 6, 14, 26, 18, 1, 9, 21, 29, 13, 5, 17, 25, 10, 2, 22, 30),
    (18, 26, 14, 6, 30, 22, 10, 2, 17, 25, 5, 13, 29, 21, 1, 9, 23, 31, 11, 3, 19, 27, 15, 7, 28, 20, 0, 8, 24, 16, 12, 4),
    (19, 27, 7, 15, 23, 31, 3, 11, 16, 24, 12, 4, 28, 20, 8, 0, 18, 26, 6, 14, 21, 29, 9, 1, 30, 22, 2, 10, 25, 17, 5, 13),
    (13, 5, 17, 25, 9, 1, 29, 21, 2, 10, 22, 30, 14, 6, 18, 26, 12, 4, 16, 24, 8, 0, 28, 20, 11, 3, 23, 31, 15, 7, 27, 19),
    (15, 7, 19, 27, 3, 11, 31, 23, 0, 8, 28, 20, 12, 4, 24, 16, 13, 5, 25, 17, 6, 14, 18, 26, 1, 9, 21, 29, 2, 10, 30, 22),
    (18, 26, 14, 6, 17, 25, 5, 13, 29, 21, 1, 9, 22, 30, 10, 2, 16, 24, 4, 12, 20, 28, 8, 0, 31, 23, 3, 11, 19, 27, 15, 7),
    (19, 27, 15, 7, 31, 23, 3, 11, 28, 20, 8, 0, 16, 24, 12, 4, 22, 30, 10, 2, 21, 29, 9, 1, 26, 18, 14, 6, 25, 17, 13, 5),
    (22, 30, 2, 10, 21, 29, 9, 1, 26, 18, 14, 6, 17, 25, 5, 13, 27, 19, 7, 15, 31, 23, 11, 3, 24, 16, 12, 4, 28, 20, 0, 8),
    (28, 20, 8, 0, 27, 19, 15, 7, 31, 23, 11, 3, 16, 24, 4, 12, 18, 26, 14, 6, 17, 25, 5, 13, 30, 22, 2, 10, 29, 21, 9, 1),
    (1, 9, 29, 21, 6, 14, 26, 18, 13, 5, 17, 25, 2, 10, 30, 22, 8, 0, 20, 28, 4, 12, 24, 16, 11, 3, 31, 23, 15, 7, 27, 19),
    (15, 7, 19, 27, 8, 0, 20, 28, 4, 12, 24, 16, 11, 3, 31, 23, 10, 2, 30, 22, 5, 13, 25, 17, 14, 6, 26, 18, 9, 1, 21, 29),
    (21, 29, 9, 1, 18, 26, 6, 14, 25, 17, 13, 5, 22, 30, 2, 10, 24, 16, 12, 4, 23, 31, 11, 3, 27, 19, 7, 15, 20, 28, 8, 0),
    (27, 19, 7, 15, 20, 28, 0, 8, 16, 24, 12, 4, 23, 31, 3, 11, 30, 22, 10, 2, 17, 25, 5, 13, 18, 26, 14, 6, 21, 29, 1, 9),
    (9, 1, 29, 21, 6, 14, 26, 18, 5, 13, 17, 25, 2, 10, 22, 30, 7, 15, 27, 19, 11, 3, 23, 31, 4, 12, 24, 16, 0, 8, 20, 28),
    (12, 4, 16, 24, 8, 0, 28, 20, 7, 15, 27, 19, 11, 3, 31, 23, 13, 5, 17, 25, 10, 2, 30, 22, 1, 9, 21, 29, 14, 6, 26, 18),
)


def color_of(row, col):
    return (col % NZ + 4 * (col // NZ) - 2 * row) % CHUNKS


def chunk_table():
    table = np.zeros((16, CHUNKS), np.int32)
    for row, places in enumerate(PLACES):
        for slot, col in enumerate(places):
            table[row, color_of(row, col)] = slot // 4
    return table


def split(index):
    row, col = divmod(index, 2 * NZ)
    return row >> 2, (col // NZ) * 2 + ((row >> 1) & 1), col % NZ, row & 1


def join(x, y, z, core):
    x, y, z = x % NX, y % NY, z % NZ
    return (x * 4 + (y & 1) * 2 + core) * 2 * NZ + (y >> 1) * NZ + z


def shift(dx=0, dy=0, dz=0):
    pairs = []
    for source in range(2 * NX * NY * NZ):
        x, y, z, core = split(source)
        pairs.append((source, join(x + dx, y + dy, z + dz, core)))
    return pairs


def spread():
    pairs = []
    for source in range(2 * NX * NY * NZ):
        x, y, z, core = split(source)
        col = (y >> 1) * NZ + z
        row, half = col // 2, col % 2
        place = PLACES[row][4 * (4 * half + x) + 2 * (y & 1) + core]
        pairs.append((source, row * 2 * NZ + place))
    return pairs


def flip_core():
    return [(source, source ^ (2 * NZ)) for source in range(2 * NX * NY * NZ)]


def send(block, pairs):
    return lax.ppermute(block, JOINT, pairs)


def hold_body(block, out):
    pass


def hold(block):
    anywhere = pl.BlockSpec(memory_space=pl.ANY)
    return pl.pallas_call(
        hold_body,
        out_shape=jax.ShapeDtypeStruct(block.shape, block.dtype),
        in_specs=[anywhere],
        out_specs=anywhere,
        input_output_aliases={0: 0},
        cost_estimate=pl.CostEstimate(flops=10**10, bytes_accessed=10**7, transcendentals=0),
    )(block)


def dequantize_body(mantissa_ref, exponent_ref, out, mantissa, exponent, sems):
    first = pltpu.make_async_copy(mantissa_ref, mantissa, sems.at[0])
    second = pltpu.make_async_copy(exponent_ref, exponent, sems.at[1])
    first.start()
    second.start()
    second.wait()
    scale = jnp.exp2(exponent[...].astype(jnp.float32))
    first.wait()
    for k in range(DEPTH // 128):
        span = slice(128 * k, 128 * (k + 1))
        out[:, span] = (mantissa[:, span].astype(jnp.float32) * scale[:, k : k + 1]).astype(jnp.bfloat16)


def dequantize(mantissa, exponent):
    anywhere = pl.BlockSpec(memory_space=pltpu.HBM)
    return pl.pallas_call(
        dequantize_body,
        out_shape=jax.ShapeDtypeStruct(mantissa.shape, jnp.bfloat16),
        in_specs=[anywhere, anywhere],
        out_specs=pl.BlockSpec(memory_space=pltpu.VMEM),
        scratch_shapes=[
            pltpu.VMEM(mantissa.shape, mantissa.dtype),
            pltpu.VMEM(exponent.shape, exponent.dtype),
            pltpu.SemaphoreType.DMA((2,)),
        ],
        compiler_params=pltpu.CompilerParams(vmem_limit_bytes=LIMIT),
    )(mantissa, exponent)


def multiply_body(first, order, columns, *rest):
    *blocks, response, held, sems = rest
    copies = []
    for block in blocks:
        for k in range(block.shape[0] // ROWS):
            slot = len(copies)
            held[slot] = lax.dot_general(
                block[ROWS * k : ROWS * (k + 1), :],
                columns[...],
                (((1,), (1,)), ((), ())),
                preferred_element_type=jnp.float32,
            )
            copies.append(pltpu.make_async_copy(held.at[slot], response.at[order[first + slot]], sems.at[slot]))
            copies[-1].start()
    for copy in copies:
        copy.wait()


def multiply(first, order, columns, blocks, response):
    count = sum(block.shape[0] for block in blocks) // ROWS
    whole = pl.BlockSpec(memory_space=pltpu.VMEM)
    anywhere = pl.BlockSpec(memory_space=pl.ANY)
    in_specs = [pl.BlockSpec(memory_space=pltpu.SMEM)] + [whole] * (1 + len(blocks))
    args = [order, columns, *blocks]
    aliases = {}

    def body(*refs):
        if response is not None:
            refs = refs[: len(args) - 1] + refs[len(args) :]
        multiply_body(first, *refs)

    if response is not None:
        in_specs.append(anywhere)
        args.append(response)
        aliases = {len(args) - 1: 0}
    return pl.pallas_call(
        body,
        out_shape=jax.ShapeDtypeStruct((CHUNKS, ROWS, COLS), jnp.float32),
        in_specs=in_specs,
        out_specs=anywhere,
        scratch_shapes=[pltpu.VMEM((count, ROWS, COLS), jnp.float32), pltpu.SemaphoreType.DMA((count,))],
        input_output_aliases=aliases,
        compiler_params=pltpu.CompilerParams(vmem_limit_bytes=LIMIT),
        cost_estimate=pl.CostEstimate(flops=count * ROWS, bytes_accessed=count * ROWS, transcendentals=0),
    )(*args)


def pair_weights(occ_level, virt_level):
    energy_gap = 0.01 * (virt_level - occ_level).astype(jnp.float32)
    return -4.0 * energy_gap / (energy_gap * energy_gap + 1.0)


def per_device(mantissa, exponent, occ_level, virt_level):
    row, col = lax.axis_index("prow"), lax.axis_index("pcol")

    own = dequantize(mantissa, exponent)
    same_x = [[4 * x + i for i in range(4)] for x in range(NX)]
    group = lax.all_gather(own, "prow", axis=0, tiled=True, axis_index_groups=same_x)

    placed = hold(send(group, spread()))
    same_core = [[2 * i + core for i in range(8)] for core in range(2)]
    eight = lax.all_to_all(
        jnp.broadcast_to(own, (8, *own.shape)), "prow", 0, 0, axis_index_groups=same_core
    )

    other = send(eight, flip_core())
    down = send(placed, shift(dz=1))
    up = send(placed, shift(dz=-1))
    over = send(placed, shift(dy=2))
    weights = pair_weights(occ_level, virt_level)
    first = jnp.where(row % 2 == 0, eight, other)
    second = jnp.where(row % 2 == 0, other, eight)
    columns = jnp.stack([first, second], axis=1).reshape(COLS, DEPTH)
    columns = (columns.astype(jnp.float32) * weights[None, :]).astype(jnp.bfloat16)
    steps = jnp.array([0, 7, 1, 4, 6, 2, 3, 5], jnp.int32)
    order = jnp.take(jnp.asarray(chunk_table()), row * CHUNKS + (color_of(row, col) + steps) % CHUNKS)
    down, up, over, columns, order = lax.optimization_barrier((down, up, over, columns, order))
    sides = jnp.concatenate([down, up], axis=0)
    over_sides = send(sides, shift(dy=2))
    down_two = send(down, shift(dz=1))
    up_two = send(up, shift(dz=-1))

    response = multiply(0, order, columns, [placed, down, up], None)
    response = multiply(3, order, columns, [over, down_two, up_two], response)
    response = multiply(6, order, columns, [over_sides], response)
    return response.reshape(CHUNKS * ROWS, COLS)


def solution(mesh):
    return jax.shard_map(
        per_device,
        mesh=mesh,
        in_specs=(P(("pcol", "prow"), None), P(("pcol", "prow"), None), P(), P()),
        out_specs=P("prow", "pcol"),
        check_vma=False,
    )
```

time: 95.8 us -> 89.6 us (0.935)
  the two profiles are of different devices: /device:TPU:186 before, /device:TPU:2 now
where the time goes in v2:
time: 89.6 us; the launch traced here: 89.1 us
  starting transfers between devices  46.9 us (52%)
  waiting for transfers between devices  23.3 us (26%)
  Pallas kernels  7.81 us (9%)
  blocking collectives  6.19 us (7%)
  local copies, waits for them, and re-layouts  3.95 us (4%)
    ppermute x8, starting transfers between devices, send(): return lax.ppermute(block, JOINT, pairs)  30.5 us
    all_to_all x1, starting transfers between devices, per_device(): lax.all_to_all(jnp.broadcast_to(own, (8, *own.shape)), 'prow', 0, 0, axis...  16.4 us
    ppermute x8, waiting for transfers between devices, send(): return lax.ppermute(block, JOINT, pairs)  13.5 us
    all_to_all x1, waiting for transfers between devices, per_device(): lax.all_to_all(jnp.broadcast_to(own, (8, *own.shape)), 'prow', 0, 0, axis...  9.77 us
    pallas_call x3, Pallas kernels, multiply(): pl.pallas_call(body, out_shape=jax.ShapeDtypeStruct((CHUNKS, ROWS, COLS),...  7.56 us
    all_gather x1, blocking collectives, per_device(): lax.all_gather(own, 'prow', axis=0, tiled=True, axis_index_groups=same_x)  6.19 us
    unnamed x15, local copies, waits for them, and re-layouts  2.4 us
  transfers between devices with their start and end apart: 9, of which 6 were waited for; matrix products, arithmetic and copies ran while one was open for 3% of the time, Pallas kernels for 6%

profile of v2, /device:TPU:2, one launch (start us, length us, event | category | flops | bytes accessed | tf_op | source)
XLA Modules:
  0.0 89.1 jit_solution(607809919430342580)
XLA Ops:
  0.0 0.8 copy.12.exponent_ref
  0.8 0.9 copy-done.2
  1.7 0.2 shard_map.64
  1.9 0.0 copy-start.6
  1.9 0.0 copy-start.3
  1.9 6.2 %all_gather.3 = bf16[160,1024]{1,0:T(8,128)(2,1)S(1)} all-gather(bf16[40,1024]{1,0:T(8,128)(2,1)S(1)} %shard_map.64), channel_id=1, replica_groups={{0,32,64,96},{128,160,192,224},{256,288,320,352},{384,416,448,480},{1,3..., dimensions={0}, use_global_device_ids=true | all-gather | bytes 409600 | tf_op jit(solution)/shard_map/all_gather | solution.py:188
  8.1 5.3 %collective-permute-start = (bf16[160,1024]{1,0:T(8,128)(2,1)S(1)}, bf16[160,1024]{1,0:T(8,128)(2,1)S(1)}, u32[]{:S(2)}, u32[]{:S(2)}) collective-permute-start(bf16[160,1024]{1,0:T(8,128)(2,1)S(1)} %all_gather.3), channel_id=1, source_target_pairs={{0,9},{1,12},{2,40},{3,38},{4,82},{5,87},{6,115},{7,114},{8,141},{... | collective-permute-start | bytes 983048 | tf_op jit(solution)/shard_map/ppermute | solution.py:83
  13.4 0.9 %broadcast_in_dim.8 = bf16[8,40,1024]{2,1,0:T(8,128)(2,1)} broadcast(bf16[40,1024]{1,0:T(8,128)(2,1)S(1)} %shard_map.64), dimensions={1,2} | broadcast | bytes 737280 | tf_op jit(solution)/shard_map/broadcast_in_dim | solution.py:193
  14.3 16.4 %all-to-all-start = ((bf16[8,40,1024]{2,1,0:T(8,128)(2,1)}), bf16[8,40,1024]{2,1,0:T(8,128)(2,1)S(1)}, u32[]{:S(2)}, u32[]{:S(2)}) async-start(bf16[8,40,1024]{2,1,0:T(8,128)(2,1)} %broadcast_in_dim.8), calls=%async_computation | async-start | bytes 1310720 | tf_op jit(solution)/shard_map/all_to_all | solution.py:192
  30.8 0.6 gather_fusion
  31.5 9.8 %all-to-all-done = bf16[8,40,1024]{2,1,0:T(8,128)(2,1)S(1)} async-done(((bf16[8,40,1024]{2,1,0:T(8,128)(2,1)}), bf16[8,40,1024]{2,1,0:T(8,128)(2,1)S(1)}, u32[]{:S(2)}, u32[]{:S(2)}) %all-to-all-start) | async-done | bytes 655392 | tf_op jit(solution)/shard_map/all_to_all | solution.py:192
  41.2 1.9 %collective-permute-start.4 = (bf16[8,40,1024]{2,1,0:T(8,128)(2,1)S(1)}, bf16[8,40,1024]{2,1,0:T(8,128)(2,1)S(1)}, u32[]{:S(2)}, u32[]{:S(2)}) collective-permute-start(bf16[8,40,1024]{2,1,0:T(8,128)(2,1)S(1)} %all-to-all-done), channel_id=1, source_target_pairs={{0,32},{1,33},{2,34},{3,35},{4,36},{5,37},{6,38},{7,39},{8,40},{9,... | collective-permute-start | bytes 1966088 | tf_op jit(solution)/shard_map/ppermute | solution.py:83
  43.2 0.0 copy-start
  43.2 0.7 copy-done
  43.9 2.8 %collective-permute-start.3 = (bf16[160,1024]{1,0:T(8,128)(2,1)}, bf16[160,1024]{1,0:T(8,128)(2,1)S(1)}, u32[]{:S(2)}, u32[]{:S(2)}) collective-permute-start(bf16[160,1024]{1,0:T(8,128)(2,1)} %shard_map.65.refs_2_), channel_id=1, source_target_pairs={{0,16},{1,17},{2,18},{3,19},{4,20},{5,21},{6,22},{7,23},{8,24},{9,... | collective-permute-start | bytes 983048 | tf_op jit(solution)/shard_map/ppermute | solution.py:83
  46.7 6.4 %collective-permute-start.2 = (bf16[160,1024]{1,0:T(8,128)(2,1)}, bf16[160,1024]{1,0:T(8,128)(2,1)S(1)}, u32[]{:S(2)}, u32[]{:S(2)}) collective-permute-start(bf16[160,1024]{1,0:T(8,128)(2,1)} %shard_map.65.refs_2_), channel_id=1, source_target_pairs={{0,15},{1,0},{2,1},{3,2},{4,3},{5,4},{6,5},{7,6},{8,7},{9,8},{10,9... | collective-permute-start | bytes 983048 | tf_op jit(solution)/shard_map/ppermute | solution.py:83
  53.1 1.9 %collective-permute-start.1 = (bf16[160,1024]{1,0:T(8,128)(2,1)}, bf16[160,1024]{1,0:T(8,128)(2,1)S(1)}, u32[]{:S(2)}, u32[]{:S(2)}) collective-permute-start(bf16[160,1024]{1,0:T(8,128)(2,1)} %shard_map.65.refs_2_), channel_id=1, source_target_pairs={{0,1},{1,2},{2,3},{3,4},{4,5},{5,6},{6,7},{7,8},{8,9},{9,10},{10,1... | collective-permute-start | bytes 983048 | tf_op jit(solution)/shard_map/ppermute | solution.py:83
  55.0 0.1 select_bitcast_fusion.1
  55.1 0.1 pad_maximum_fusion
  55.3 0.4 fusion.refs_1_
  55.7 0.0 copy-start.1
  55.7 1.9 %collective-permute-done.3.refs_2_ = bf16[160,1024]{1,0:T(8,128)(2,1)S(1)} collective-permute-done((bf16[160,1024]{1,0:T(8,128)(2,1)}, bf16[160,1024]{1,0:T(8,128)(2,1)S(1)}, u32[]{:S(2)}, u32[]{:S(2)}) %collective-permute-start.3) | collective-permute-done | bytes 327712 | tf_op jit(solution)/shard_map/ppermute | solution.py:83
  57.6 3.4 %collective-permute-done.2.refs_4_ = bf16[160,1024]{1,0:T(8,128)(2,1)S(1)} collective-permute-done((bf16[160,1024]{1,0:T(8,128)(2,1)}, bf16[160,1024]{1,0:T(8,128)(2,1)S(1)}, u32[]{:S(2)}, u32[]{:S(2)}) %collective-permute-start.2) | collective-permute-done | bytes 327712 | tf_op jit(solution)/shard_map/ppermute | solution.py:83
  61.0 5.2 %collective-permute-done.1.refs_3_ = bf16[160,1024]{1,0:T(8,128)(2,1)S(1)} collective-permute-done((bf16[160,1024]{1,0:T(8,128)(2,1)}, bf16[160,1024]{1,0:T(8,128)(2,1)S(1)}, u32[]{:S(2)}, u32[]{:S(2)}) %collective-permute-start.1) | collective-permute-done | bytes 327712 | tf_op jit(solution)/shard_map/ppermute | solution.py:83
  66.3 5.1 %collective-permute-start.5 = (bf16[320,1024]{1,0:T(8,128)(2,1)S(1)}, bf16[320,1024]{1,0:T(8,128)(2,1)S(1)}, u32[]{:S(2)}, u32[]{:S(2)}) collective-permute-start(bf16[320,1024]{1,0:T(8,128)(2,1)S(1)} %pad_maximum_fusion.1), channel_id=1, source_target_pairs={{0,16},{1,17},{2,18},{3,19},{4,20},{5,21},{6,22},{7,23},{8,24},{9,... | collective-permute-start | bytes 1966088 | tf_op jit(solution)/shard_map/ppermute | solution.py:83
  71.5 1.9 %collective-permute-start.6 = (bf16[160,1024]{1,0:T(8,128)(2,1)S(1)}, bf16[160,1024]{1,0:T(8,128)(2,1)S(1)}, u32[]{:S(2)}, u32[]{:S(2)}) collective-permute-start(bf16[160,1024]{1,0:T(8,128)(2,1)S(1)} %collective-permute-done.1.refs_3_), channel_id=1, source_target_pairs={{0,1},{1,2},{2,3},{3,4},{4,5},{5,6},{6,7},{7,8},{8,9},{9,10},{10,1... | collective-permute-start | bytes 983048 | tf_op jit(solution)/shard_map/ppermute | solution.py:83
  73.4 5.1 %collective-permute-start.7 = (bf16[160,1024]{1,0:T(8,128)(2,1)S(1)}, bf16[160,1024]{1,0:T(8,128)(2,1)S(1)}, u32[]{:S(2)}, u32[]{:S(2)}) collective-permute-start(bf16[160,1024]{1,0:T(8,128)(2,1)S(1)} %collective-permute-done.2.refs_4_), channel_id=1, source_target_pairs={{0,15},{1,0},{2,1},{3,2},{4,3},{5,4},{6,5},{7,6},{8,7},{9,8},{10,9... | collective-permute-start | bytes 983048 | tf_op jit(solution)/shard_map/ppermute | solution.py:83
  78.5 2.6 %shard_map.66.refs_5_ = f32[8,160,640]{2,1,0:T(8,128)} custom-call(s32[8]{0:T(128)S(1)} %and_select_fusion.refs_0_, bf16[640,1024]{1,0:T(8,128)(2,1)S(1)} %fusion.refs_1_, bf16[160,1024]{1,0:T(8,128)(2,1)S(1)} %copy-done.1, bf16[160,1024]{1,0:T(8,128)(2,1)S(1)} %collective-permute-done.1.refs_3_, bf16[160,1024]{1,0:T(8,128)(2,1)S(1)} %collective-permute-done.2.refs_4_), custom_call_target="tpu_custom_call" | custom-call | flops 480 | bytes 480 | tf_op jit(solution)/shard_map/pallas_call | solution.py:166
  81.2 1.8 %collective-permute-done.6.refs_3_ = bf16[160,1024]{1,0:T(8,128)(2,1)S(1)} collective-permute-done((bf16[160,1024]{1,0:T(8,128)(2,1)S(1)}, bf16[160,1024]{1,0:T(8,128)(2,1)S(1)}, u32[]{:S(2)}, u32[]{:S(2)}) %collective-permute-start.6) | collective-permute-done | bytes 327712 | tf_op jit(solution)/shard_map/ppermute | solution.py:83
  83.0 1.2 %collective-permute-done.7.refs_4_ = bf16[160,1024]{1,0:T(8,128)(2,1)S(1)} collective-permute-done((bf16[160,1024]{1,0:T(8,128)(2,1)S(1)}, bf16[160,1024]{1,0:T(8,128)(2,1)S(1)}, u32[]{:S(2)}, u32[]{:S(2)}) %collective-permute-start.7) | collective-permute-done | bytes 327712 | tf_op jit(solution)/shard_map/ppermute | solution.py:83
  84.2 2.6 %shard_map.67.refs_3_ = f32[8,160,640]{2,1,0:T(8,128)} custom-call(s32[8]{0:T(128)S(1)} %and_select_fusion.refs_0_, bf16[640,1024]{1,0:T(8,128)(2,1)S(1)} %fusion.refs_1_, bf16[160,1024]{1,0:T(8,128)(2,1)S(1)} %collective-permute-done.3.refs_2_, bf16[160,1024]{1,0:T(8,128)(2,1)S(1)} %collective-permute-done.6.refs_3_, ...), custom_call_target="tpu_custom_call", output_to_operand_aliasing={{}: (5, {})} | custom-call | flops 480 | bytes 480 | tf_op jit(solution)/shard_map/pallas_call | solution.py:166
  86.8 2.3 %shard_map.68 = f32[8,160,640]{2,1,0:T(8,128)} custom-call(s32[8]{0:T(128)S(1)} %and_select_fusion.refs_0_, bf16[640,1024]{1,0:T(8,128)(2,1)S(1)} %fusion.refs_1_, bf16[320,1024]{1,0:T(8,128)(2,1)S(1)} %collective-permute-done.5.refs_2_, f32[8,160,640]{2,1,0:T(8,128)} %shard_map.67.refs_3_), custom_call_target="tpu_custom_call", output_to_operand_aliasing={{}: (3, {})} | custom-call | flops 320 | bytes 320 | tf_op jit(solution)/shard_map/pallas_call | solution.py:166
  (17 shorter events, 0.1 us)
Async XLA Ops:
  0.8 0.9 copy-start.2
  1.9 28.8 %copy-start.6 = (s32[8]{0:T(128)S(1)}, s32[8]{0:T(128)}, u32[]{:S(2)}) copy-start(s32[8]{0:T(128)} %constant.92.clone) | copy-start | bytes 100
  1.9 28.8 %copy-start.3 = (s32[128]{0:T(128)S(1)}, s32[128]{0:T(128)}, u32[]{:S(2)}) copy-start(s32[128]{0:T(128)} %constant.96) | copy-start | bytes 1540
  8.1 23.3 %copy-start.4 = (s32[1024]{0:T(1024)S(1)}, s32[1024]{0:T(1024)}, u32[]{:S(2)}) copy-start(s32[1024]{0:T(1024)} %param.9) | copy-start | bytes 12292
  8.1 23.3 %copy-start.5 = (s32[1024]{0:T(1024)S(1)}, s32[1024]{0:T(1024)}, u32[]{:S(2)}) copy-start(s32[1024]{0:T(1024)} %param.8) | copy-start | bytes 12292
  8.1 35.0 %collective-permute-start = (bf16[160,1024]{1,0:T(8,128)(2,1)S(1)}, bf16[160,1024]{1,0:T(8,128)(2,1)S(1)}, u32[]{:S(2)}, u32[]{:S(2)}) collective-permute-start(bf16[160,1024]{1,0:T(8,128)(2,1)S(1)} %all_gather.3), channel_id=1, source_target_pairs={{0,9},{1,12},{2,40},{3,38},{4,82},{5,87},{6,115},{7,114},{8,141},{... | collective-permute-start | bytes 983048 | tf_op jit(solution)/shard_map/ppermute | solution.py:83
  14.3 26.9 %all-to-all-start = ((bf16[8,40,1024]{2,1,0:T(8,128)(2,1)}), bf16[8,40,1024]{2,1,0:T(8,128)(2,1)S(1)}, u32[]{:S(2)}, u32[]{:S(2)}) async-start(bf16[8,40,1024]{2,1,0:T(8,128)(2,1)} %broadcast_in_dim.8), calls=%async_computation | async-start | bytes 1310720 | tf_op jit(solution)/shard_map/all_to_all | solution.py:192
  41.2 13.8 %collective-permute-start.4 = (bf16[8,40,1024]{2,1,0:T(8,128)(2,1)S(1)}, bf16[8,40,1024]{2,1,0:T(8,128)(2,1)S(1)}, u32[]{:S(2)}, u32[]{:S(2)}) collective-permute-start(bf16[8,40,1024]{2,1,0:T(8,128)(2,1)S(1)} %all-to-all-done), channel_id=1, source_target_pairs={{0,32},{1,33},{2,34},{3,35},{4,36},{5,37},{6,38},{7,39},{8,40},{9,... | collective-permute-start | bytes 1966088 | tf_op jit(solution)/shard_map/ppermute | solution.py:83
  43.2 0.7 copy-start
  43.9 13.7 %collective-permute-start.3 = (bf16[160,1024]{1,0:T(8,128)(2,1)}, bf16[160,1024]{1,0:T(8,128)(2,1)S(1)}, u32[]{:S(2)}, u32[]{:S(2)}) collective-permute-start(bf16[160,1024]{1,0:T(8,128)(2,1)} %shard_map.65.refs_2_), channel_id=1, source_target_pairs={{0,16},{1,17},{2,18},{3,19},{4,20},{5,21},{6,22},{7,23},{8,24},{9,... | collective-permute-start | bytes 983048 | tf_op jit(solution)/shard_map/ppermute | solution.py:83
  46.7 14.4 %collective-permute-start.2 = (bf16[160,1024]{1,0:T(8,128)(2,1)}, bf16[160,1024]{1,0:T(8,128)(2,1)S(1)}, u32[]{:S(2)}, u32[]{:S(2)}) collective-permute-start(bf16[160,1024]{1,0:T(8,128)(2,1)} %shard_map.65.refs_2_), channel_id=1, source_target_pairs={{0,15},{1,0},{2,1},{3,2},{4,3},{5,4},{6,5},{7,6},{8,7},{9,8},{10,9... | collective-permute-start | bytes 983048 | tf_op jit(solution)/shard_map/ppermute | solution.py:83
  53.1 13.1 %collective-permute-start.1 = (bf16[160,1024]{1,0:T(8,128)(2,1)}, bf16[160,1024]{1,0:T(8,128)(2,1)S(1)}, u32[]{:S(2)}, u32[]{:S(2)}) collective-permute-start(bf16[160,1024]{1,0:T(8,128)(2,1)} %shard_map.65.refs_2_), channel_id=1, source_target_pairs={{0,1},{1,2},{2,3},{3,4},{4,5},{5,6},{6,7},{7,8},{8,9},{9,10},{10,1... | collective-permute-start | bytes 983048 | tf_op jit(solution)/shard_map/ppermute | solution.py:83
  55.7 22.8 %copy-start.1 = (bf16[160,1024]{1,0:T(8,128)(2,1)S(1)}, bf16[160,1024]{1,0:T(8,128)(2,1)}, u32[]{:S(2)}) copy-start(bf16[160,1024]{1,0:T(8,128)(2,1)} %shard_map.65.refs_2_) | copy-start | bytes 983044
  66.3 20.5 %collective-permute-start.5 = (bf16[320,1024]{1,0:T(8,128)(2,1)S(1)}, bf16[320,1024]{1,0:T(8,128)(2,1)S(1)}, u32[]{:S(2)}, u32[]{:S(2)}) collective-permute-start(bf16[320,1024]{1,0:T(8,128)(2,1)S(1)} %pad_maximum_fusion.1), channel_id=1, source_target_pairs={{0,16},{1,17},{2,18},{3,19},{4,20},{5,21},{6,22},{7,23},{8,24},{9,... | collective-permute-start | bytes 1966088 | tf_op jit(solution)/shard_map/ppermute | solution.py:83
  71.5 11.5 %collective-permute-start.6 = (bf16[160,1024]{1,0:T(8,128)(2,1)S(1)}, bf16[160,1024]{1,0:T(8,128)(2,1)S(1)}, u32[]{:S(2)}, u32[]{:S(2)}) collective-permute-start(bf16[160,1024]{1,0:T(8,128)(2,1)S(1)} %collective-permute-done.1.refs_3_), channel_id=1, source_target_pairs={{0,1},{1,2},{2,3},{3,4},{4,5},{5,6},{6,7},{7,8},{8,9},{9,10},{10,1... | collective-permute-start | bytes 983048 | tf_op jit(solution)/shard_map/ppermute | solution.py:83
  73.4 10.8 %collective-permute-start.7 = (bf16[160,1024]{1,0:T(8,128)(2,1)S(1)}, bf16[160,1024]{1,0:T(8,128)(2,1)S(1)}, u32[]{:S(2)}, u32[]{:S(2)}) collective-permute-start(bf16[160,1024]{1,0:T(8,128)(2,1)S(1)} %collective-permute-done.2.refs_4_), channel_id=1, source_target_pairs={{0,15},{1,0},{2,1},{3,2},{4,3},{5,4},{6,5},{7,6},{8,7},{9,8},{10,9... | collective-permute-start | bytes 983048 | tf_op jit(solution)/shard_map/ppermute | solution.py:83

commit v3 on v2

--- a/solution.py
+++ b/solution.py
@@ -75,28 +75,8 @@
     return pairs
 
 
-def flip_core():
-    return [(source, source ^ (2 * NZ)) for source in range(2 * NX * NY * NZ)]
-
-
 def send(block, pairs):
     return lax.ppermute(block, JOINT, pairs)
-
-
-def hold_body(block, out):
-    pass
-
-
-def hold(block):
-    anywhere = pl.BlockSpec(memory_space=pl.ANY)
-    return pl.pallas_call(
-        hold_body,
-        out_shape=jax.ShapeDtypeStruct(block.shape, block.dtype),
-        in_specs=[anywhere],
-        out_specs=anywhere,
-        input_output_aliases={0: 0},
-        cost_estimate=pl.CostEstimate(flops=10**10, bytes_accessed=10**7, transcendentals=0),
-    )(block)
 
 
 def dequantize_body(mantissa_ref, exponent_ref, out, mantissa, exponent, sems):
@@ -105,7 +85,7 @@
     first.start()
     second.start()
     second.wait()
-    scale = jnp.exp2(exponent[...].astype(jnp.float32))
+    scale = jnp.exp2(exponent[...].astype(jnp.float32)).T
     first.wait()
     for k in range(DEPTH // 128):
         span = slice(128 * k, 128 * (k + 1))
@@ -121,11 +101,29 @@
         out_specs=pl.BlockSpec(memory_space=pltpu.VMEM),
         scratch_shapes=[
             pltpu.VMEM(mantissa.shape, mantissa.dtype),
-            pltpu.VMEM(exponent.shape, exponent.dtype),
+            pltpu.VMEM(exponent.shape[::-1], exponent.dtype),
             pltpu.SemaphoreType.DMA((2,)),
         ],
         compiler_params=pltpu.CompilerParams(vmem_limit_bytes=LIMIT),
-    )(mantissa, exponent)
+    )(mantissa, exponent.T)
+
+
+def scale_body(weights, rows, out):
+    for k in range(DEPTH // 256):
+        span = slice(256 * k, 256 * (k + 1))
+        out[span, :] = (rows[:, span].astype(jnp.float32) * weights[:, span]).astype(jnp.bfloat16).T
+
+
+def scale(weights, rows):
+    whole = pl.BlockSpec(memory_space=pltpu.VMEM)
+    return pl.pallas_call(
+        scale_body,
+        out_shape=jax.ShapeDtypeStruct((DEPTH, COLS), jnp.bfloat16),
+        in_specs=[whole, whole],
+        out_specs=whole,
+        compiler_params=pltpu.CompilerParams(vmem_limit_bytes=LIMIT),
+        cost_estimate=pl.CostEstimate(flops=COLS, bytes_accessed=COLS, transcendentals=0),
+    )(weights, rows)
 
 
 def multiply_body(first, order, columns, *rest):
@@ -134,11 +132,8 @@
     for block in blocks:
         for k in range(block.shape[0] // ROWS):
             slot = len(copies)
-            held[slot] = lax.dot_general(
-                block[ROWS * k : ROWS * (k + 1), :],
-                columns[...],
-                (((1,), (1,)), ((), ())),
-                preferred_element_type=jnp.float32,
+            held[slot] = jnp.dot(
+                block[ROWS * k : ROWS * (k + 1), :], columns[...], preferred_element_type=jnp.float32
             )
             copies.append(pltpu.make_async_copy(held.at[slot], response.at[order[first + slot]], sems.at[slot]))
             copies[-1].start()
@@ -187,32 +182,26 @@
     same_x = [[4 * x + i for i in range(4)] for x in range(NX)]
     group = lax.all_gather(own, "prow", axis=0, tiled=True, axis_index_groups=same_x)
 
-    placed = hold(send(group, spread()))
-    same_core = [[2 * i + core for i in range(8)] for core in range(2)]
-    eight = lax.all_to_all(
-        jnp.broadcast_to(own, (8, *own.shape)), "prow", 0, 0, axis_index_groups=same_core
+    placed = send(group, spread())
+    along_x = [[4 * x + i for x in range(NX)] for i in range(4)]
+    groups = lax.all_to_all(
+        jnp.broadcast_to(group, (NX, *group.shape)), "prow", 0, 0, axis_index_groups=along_x
     )
-
-    other = send(eight, flip_core())
     down = send(placed, shift(dz=1))
     up = send(placed, shift(dz=-1))
     over = send(placed, shift(dy=2))
-    weights = pair_weights(occ_level, virt_level)
-    first = jnp.where(row % 2 == 0, eight, other)
-    second = jnp.where(row % 2 == 0, other, eight)
-    columns = jnp.stack([first, second], axis=1).reshape(COLS, DEPTH)
-    columns = (columns.astype(jnp.float32) * weights[None, :]).astype(jnp.bfloat16)
+    weights = pair_weights(occ_level, virt_level)[None, :]
+    columns = scale(weights, groups.reshape(COLS, DEPTH))
     steps = jnp.array([0, 7, 1, 4, 6, 2, 3, 5], jnp.int32)
     order = jnp.take(jnp.asarray(chunk_table()), row * CHUNKS + (color_of(row, col) + steps) % CHUNKS)
-    down, up, over, columns, order = lax.optimization_barrier((down, up, over, columns, order))
+    down, up, over, order = lax.optimization_barrier((down, up, over, order))
     sides = jnp.concatenate([down, up], axis=0)
     over_sides = send(sides, shift(dy=2))
     down_two = send(down, shift(dz=1))
     up_two = send(up, shift(dz=-1))
 
-    response = multiply(0, order, columns, [placed, down, up], None)
-    response = multiply(3, order, columns, [over, down_two, up_two], response)
-    response = multiply(6, order, columns, [over_sides], response)
+    response = multiply(0, order, columns, [placed, down, up, over], None)
+    response = multiply(4, order, columns, [down_two, up_two, over_sides], response)
     return response.reshape(CHUNKS * ROWS, COLS)
 
 

time: 89.6 us -> 87 us (0.971)
  waiting for transfers between devices: 23.3 us -> 18.2 us
  starting transfers between devices: 46.9 us -> 51.3 us
  Pallas kernels: 7.81 us -> 6.32 us
    all_to_all x1, waiting for transfers between devices: 9.77 us -> 0.01 us  [per_device(): lax.all_to_all(jnp.broadcast_to(group, (NX, *group.shape)), 'prow', 0, 0,...]
    ppermute x8 -> x7, starting transfers between devices: 30.5 us -> 37 us  [send(): return lax.ppermute(block, JOINT, pairs)]
    ppermute x8 -> x7, waiting for transfers between devices: 13.5 us -> 18.2 us  [send(): return lax.ppermute(block, JOINT, pairs)]
    all_to_all x1, starting transfers between devices: 16.4 us -> 14.3 us  [per_device(): lax.all_to_all(jnp.broadcast_to(group, (NX, *group.shape)), 'prow', 0, 0,...]
    pallas_call x3 -> x2, Pallas kernels: 7.56 us -> 5.63 us  [multiply(): pl.pallas_call(body, out_shape=jax.ShapeDtypeStruct((CHUNKS, ROWS, COLS),...]
    unnamed x15 -> x12, local copies, waits for them, and re-layouts: 2.4 us -> 1.59 us
  transfers between devices with their start and end apart: 9 -> 8, of which waited for: 6 -> 5; matrix products, arithmetic and copies ran while one was open for 3% -> 3% of each run, Pallas kernels for 6% -> 3%
where the time goes in v3:
time: 87 us; the launch traced here: 86.5 us
  starting transfers between devices  51.3 us (59%)
  waiting for transfers between devices  18.2 us (21%)
  Pallas kernels  6.32 us (7%)
  blocking collectives  6.19 us (7%)
  local copies, waits for them, and re-layouts  3.45 us (4%)
  other arithmetic  0.93 us (1%)
    ppermute x7, starting transfers between devices, send(): return lax.ppermute(block, JOINT, pairs)  37 us
    ppermute x7, waiting for transfers between devices, send(): return lax.ppermute(block, JOINT, pairs)  18.2 us
    all_to_all x1, starting transfers between devices, per_device(): lax.all_to_all(jnp.broadcast_to(group, (NX, *group.shape)), 'prow', 0, 0,...  14.3 us
    all_gather x1, blocking collectives, per_device(): lax.all_gather(own, 'prow', axis=0, tiled=True, axis_index_groups=same_x)  6.19 us
    pallas_call x2, Pallas kernels, multiply(): pl.pallas_call(body, out_shape=jax.ShapeDtypeStruct((CHUNKS, ROWS, COLS),...  5.63 us
  transfers between devices with their start and end apart: 8, of which 5 were waited for; matrix products, arithmetic and copies ran while one was open for 3% of the time, Pallas kernels for 3%

profile of v3, /device:TPU:2, one launch (start us, length us, event | category | flops | bytes accessed | tf_op | source)
XLA Modules:
  0.0 86.5 jit_solution(4004749281103211317)
XLA Ops:
  0.0 0.0 copy-start
  0.0 0.9 %copy-done = bf16[40,1024]{1,0:T(8,128)(2,1)S(1)} copy-done((bf16[40,1024]{1,0:T(8,128)(2,1)S(1)}, bf16[40,1024]{1,0:T(8,128)(2,1)}, u32[]{:S(2)}) %copy-start) | copy-done | bytes 81944
  0.9 0.0 copy-start.1
  0.9 0.7 copy-done.1
  1.6 0.3 shard_map.64
  1.9 6.2 %all_gather.3 = bf16[160,1024]{1,0:T(8,128)(2,1)S(1)} all-gather(bf16[40,1024]{1,0:T(8,128)(2,1)S(1)} %shard_map.64), channel_id=1, replica_groups={{0,32,64,96},{128,160,192,224},{256,288,320,352},{384,416,448,480},{1,3..., dimensions={0}, use_global_device_ids=true | all-gather | bytes 409600 | tf_op jit(solution)/shard_map/all_gather | solution.py:183
  8.1 5.1 %collective-permute-start = (bf16[160,1024]{1,0:T(8,128)(2,1)S(1)}, bf16[160,1024]{1,0:T(8,128)(2,1)S(1)}, u32[]{:S(2)}, u32[]{:S(2)}) collective-permute-start(bf16[160,1024]{1,0:T(8,128)(2,1)S(1)} %all_gather.3), channel_id=1, source_target_pairs={{0,9},{1,12},{2,40},{3,38},{4,82},{5,87},{6,115},{7,114},{8,141},{... | collective-permute-start | bytes 983048 | tf_op jit(solution)/shard_map/ppermute | solution.py:79
  13.2 1.2 %broadcast_in_dim.12 = bf16[4,160,1024]{2,1,0:T(8,128)(2,1)} broadcast(bf16[160,1024]{1,0:T(8,128)(2,1)S(1)} %all_gather.3), dimensions={1,2} | broadcast | bytes 1638400 | tf_op jit(solution)/shard_map/broadcast_in_dim | solution.py:188
  14.4 14.3 %all-to-all-start = ((bf16[4,160,1024]{2,1,0:T(8,128)(2,1)}), bf16[4,160,1024]{2,1,0:T(8,128)(2,1)S(1)}, u32[]{:S(2)}, u32[]{:S(2)}) async-start(bf16[4,160,1024]{2,1,0:T(8,128)(2,1)} %broadcast_in_dim.12), calls=%async_computation | async-start | bytes 2621440 | tf_op jit(solution)/shard_map/all_to_all | solution.py:187
  28.8 0.0 copy-done.5
  28.8 0.0 collective-permute-done.refs_2_
  28.8 10.2 %collective-permute-start.3 = (bf16[160,1024]{1,0:T(8,128)(2,1)S(1)}, bf16[160,1024]{1,0:T(8,128)(2,1)S(1)}, u32[]{:S(2)}, u32[]{:S(2)}) collective-permute-start(bf16[160,1024]{1,0:T(8,128)(2,1)S(1)} %collective-permute-done.refs_2_), channel_id=1, source_target_pairs={{0,16},{1,17},{2,18},{3,19},{4,20},{5,21},{6,22},{7,23},{8,24},{9,... | collective-permute-start | bytes 983048 | tf_op jit(solution)/shard_map/ppermute | solution.py:79
  39.0 10.5 %collective-permute-start.2 = (bf16[160,1024]{1,0:T(8,128)(2,1)S(1)}, bf16[160,1024]{1,0:T(8,128)(2,1)S(1)}, u32[]{:S(2)}, u32[]{:S(2)}) collective-permute-start(bf16[160,1024]{1,0:T(8,128)(2,1)S(1)} %collective-permute-done.refs_2_), channel_id=1, source_target_pairs={{0,15},{1,0},{2,1},{3,2},{4,3},{5,4},{6,5},{7,6},{8,7},{9,8},{10,9... | collective-permute-start | bytes 983048 | tf_op jit(solution)/shard_map/ppermute | solution.py:79
  49.5 1.9 %collective-permute-start.1 = (bf16[160,1024]{1,0:T(8,128)(2,1)S(1)}, bf16[160,1024]{1,0:T(8,128)(2,1)S(1)}, u32[]{:S(2)}, u32[]{:S(2)}) collective-permute-start(bf16[160,1024]{1,0:T(8,128)(2,1)S(1)} %collective-permute-done.refs_2_), channel_id=1, source_target_pairs={{0,1},{1,2},{2,3},{3,4},{4,5},{5,6},{6,7},{7,8},{8,9},{9,10},{10,1... | collective-permute-start | bytes 983048 | tf_op jit(solution)/shard_map/ppermute | solution.py:79
  51.4 0.0 copy-done.2
  51.4 0.6 gather_fusion
  52.1 0.0 collective-permute-done.3.refs_5_
  52.1 5.2 %collective-permute-done.2.refs_4_ = bf16[160,1024]{1,0:T(8,128)(2,1)S(1)} collective-permute-done((bf16[160,1024]{1,0:T(8,128)(2,1)S(1)}, bf16[160,1024]{1,0:T(8,128)(2,1)S(1)}, u32[]{:S(2)}, u32[]{:S(2)}) %collective-permute-start.2) | collective-permute-done | bytes 327712 | tf_op jit(solution)/shard_map/ppermute | solution.py:79
  57.3 5.3 %collective-permute-done.1.refs_3_ = bf16[160,1024]{1,0:T(8,128)(2,1)S(1)} collective-permute-done((bf16[160,1024]{1,0:T(8,128)(2,1)S(1)}, bf16[160,1024]{1,0:T(8,128)(2,1)S(1)}, u32[]{:S(2)}, u32[]{:S(2)}) %collective-permute-start.1) | collective-permute-done | bytes 327712 | tf_op jit(solution)/shard_map/ppermute | solution.py:79
  62.6 0.9 %pad_maximum_fusion = bf16[320,1024]{1,0:T(8,128)(2,1)} fusion(bf16[160,1024]{1,0:T(8,128)(2,1)S(1)} %collective-permute-done.2.refs_4_, bf16[160,1024]{1,0:T(8,128)(2,1)S(1)} %collective-permute-done.1.refs_3_), kind=kLoop, calls=%fused_computation.1 | loop fusion | flops 1310720 | bytes 1310720 | tf_op jit(solution)/shard_map/concatenate | solution.py:198
  63.5 2.2 %collective-permute-start.6 = (bf16[320,1024]{1,0:T(8,128)(2,1)}, bf16[320,1024]{1,0:T(8,128)(2,1)S(1)}, u32[]{:S(2)}, u32[]{:S(2)}) collective-permute-start(bf16[320,1024]{1,0:T(8,128)(2,1)} %pad_maximum_fusion), channel_id=1, source_target_pairs={{0,16},{1,17},{2,18},{3,19},{4,20},{5,21},{6,22},{7,23},{8,24},{9,... | collective-permute-start | bytes 1966088 | tf_op jit(solution)/shard_map/ppermute | solution.py:79
  65.7 1.9 %collective-permute-start.4 = (bf16[160,1024]{1,0:T(8,128)(2,1)S(1)}, bf16[160,1024]{1,0:T(8,128)(2,1)}, u32[]{:S(2)}, u32[]{:S(2)}) collective-permute-start(bf16[160,1024]{1,0:T(8,128)(2,1)S(1)} %collective-permute-done.1.refs_3_), channel_id=1, source_target_pairs={{0,1},{1,2},{2,3},{3,4},{4,5},{5,6},{6,7},{7,8},{8,9},{9,10},{10,1... | collective-permute-start | bytes 983048 | tf_op jit(solution)/shard_map/ppermute | solution.py:79
  67.6 5.1 %collective-permute-start.5 = (bf16[160,1024]{1,0:T(8,128)(2,1)S(1)}, bf16[160,1024]{1,0:T(8,128)(2,1)}, u32[]{:S(2)}, u32[]{:S(2)}) collective-permute-start(bf16[160,1024]{1,0:T(8,128)(2,1)S(1)} %collective-permute-done.2.refs_4_), channel_id=1, source_target_pairs={{0,15},{1,0},{2,1},{3,2},{4,3},{5,4},{6,5},{7,6},{8,7},{9,8},{10,9... | collective-permute-start | bytes 983048 | tf_op jit(solution)/shard_map/ppermute | solution.py:79
  72.8 0.0 copy-done.3
  72.8 0.0 copy-done.4
  72.8 0.0 all-to-all-done
  72.8 0.4 shard_map.65.refs_1_
  73.2 2.5 %shard_map.66.refs_5_ = f32[8,160,640]{2,1,0:T(8,128)} custom-call(s32[8]{0:T(128)S(1)} %and_select_fusion.refs_0_, bf16[1024,640]{1,0:T(8,128)(2,1)S(1)} %shard_map.65.refs_1_, bf16[160,1024]{1,0:T(8,128)(2,1)S(1)} %collective-permute-done.refs_2_, bf16[160,1024]{1,0:T(8,128)(2,1)S(1)} %collective-permute-done.1.refs_3_, ...), custom_call_target="tpu_custom_call" | custom-call | flops 640 | bytes 640 | tf_op jit(solution)/shard_map/pallas_call | solution.py:161
  75.8 2.3 %collective-permute-done.4.refs_2_ = bf16[160,1024]{1,0:T(8,128)(2,1)} collective-permute-done((bf16[160,1024]{1,0:T(8,128)(2,1)S(1)}, bf16[160,1024]{1,0:T(8,128)(2,1)}, u32[]{:S(2)}, u32[]{:S(2)}) %collective-permute-start.4) | collective-permute-done | bytes 327712 | tf_op jit(solution)/shard_map/ppermute | solution.py:79
  78.1 1.1 %collective-permute-done.5.refs_3_ = bf16[160,1024]{1,0:T(8,128)(2,1)} collective-permute-done((bf16[160,1024]{1,0:T(8,128)(2,1)S(1)}, bf16[160,1024]{1,0:T(8,128)(2,1)}, u32[]{:S(2)}, u32[]{:S(2)}) %collective-permute-start.5) | collective-permute-done | bytes 327712 | tf_op jit(solution)/shard_map/ppermute | solution.py:79
  79.2 4.2 %collective-permute-done.6.refs_4_ = bf16[320,1024]{1,0:T(8,128)(2,1)S(1)} collective-permute-done((bf16[320,1024]{1,0:T(8,128)(2,1)}, bf16[320,1024]{1,0:T(8,128)(2,1)S(1)}, u32[]{:S(2)}, u32[]{:S(2)}) %collective-permute-start.6) | collective-permute-done | bytes 655392 | tf_op jit(solution)/shard_map/ppermute | solution.py:79
  83.4 3.1 %shard_map.67 = f32[8,160,640]{2,1,0:T(8,128)} custom-call(s32[8]{0:T(128)S(1)} %and_select_fusion.refs_0_, bf16[1024,640]{1,0:T(8,128)(2,1)S(1)} %shard_map.65.refs_1_, bf16[160,1024]{1,0:T(8,128)(2,1)} %collective-permute-done.4.refs_2_, bf16[160,1024]{1,0:T(8,128)(2,1)} %collective-permute-done.5.refs_3_, ...), custom_call_target="tpu_custom_call", output_to_operand_aliasing={{}: (5, {})} | custom-call | flops 640 | bytes 640 | tf_op jit(solution)/shard_map/pallas_call | solution.py:161
  (8 shorter events, 0.1 us)
Async XLA Ops:
  0.0 0.9 %copy-start = (bf16[40,1024]{1,0:T(8,128)(2,1)S(1)}, bf16[40,1024]{1,0:T(8,128)(2,1)}, u32[]{:S(2)}) copy-start(bf16[40,1024]{1,0:T(8,128)(2,1)} %mantissa_ref.1) | copy-start | bytes 245764
  0.9 0.7 copy-start.1
  8.1 20.7 %collective-permute-start = (bf16[160,1024]{1,0:T(8,128)(2,1)S(1)}, bf16[160,1024]{1,0:T(8,128)(2,1)S(1)}, u32[]{:S(2)}, u32[]{:S(2)}) collective-permute-start(bf16[160,1024]{1,0:T(8,128)(2,1)S(1)} %all_gather.3), channel_id=1, source_target_pairs={{0,9},{1,12},{2,40},{3,38},{4,82},{5,87},{6,115},{7,114},{8,141},{... | collective-permute-start | bytes 983048 | tf_op jit(solution)/shard_map/ppermute | solution.py:79
  14.4 14.3 %copy-start.5 = (s32[8]{0:T(128)S(1)}, s32[8]{0:T(128)}, u32[]{:S(2)}) copy-start(s32[8]{0:T(128)} %constant.82.clone) | copy-start | bytes 100
  14.4 37.0 %copy-start.2 = (s32[128]{0:T(128)S(1)}, s32[128]{0:T(128)}, u32[]{:S(2)}) copy-start(s32[128]{0:T(128)} %constant.86) | copy-start | bytes 1540
  14.4 58.4 %all-to-all-start = ((bf16[4,160,1024]{2,1,0:T(8,128)(2,1)}), bf16[4,160,1024]{2,1,0:T(8,128)(2,1)S(1)}, u32[]{:S(2)}, u32[]{:S(2)}) async-start(bf16[4,160,1024]{2,1,0:T(8,128)(2,1)} %broadcast_in_dim.12), calls=%async_computation | async-start | bytes 2621440 | tf_op jit(solution)/shard_map/all_to_all | solution.py:187
  28.7 44.0 %copy-start.3 = (s32[1024]{0:T(1024)S(1)}, s32[1024]{0:T(1024)}, u32[]{:S(2)}) copy-start(s32[1024]{0:T(1024)} %param.9) | copy-start | bytes 12292
  28.7 44.0 %copy-start.4 = (s32[1024]{0:T(1024)S(1)}, s32[1024]{0:T(1024)}, u32[]{:S(2)}) copy-start(s32[1024]{0:T(1024)} %param.8) | copy-start | bytes 12292
  28.8 23.3 %collective-permute-start.3 = (bf16[160,1024]{1,0:T(8,128)(2,1)S(1)}, bf16[160,1024]{1,0:T(8,128)(2,1)S(1)}, u32[]{:S(2)}, u32[]{:S(2)}) collective-permute-start(bf16[160,1024]{1,0:T(8,128)(2,1)S(1)} %collective-permute-done.refs_2_), channel_id=1, source_target_pairs={{0,16},{1,17},{2,18},{3,19},{4,20},{5,21},{6,22},{7,23},{8,24},{9,... | collective-permute-start | bytes 983048 | tf_op jit(solution)/shard_map/ppermute | solution.py:79
  39.0 18.3 %collective-permute-start.2 = (bf16[160,1024]{1,0:T(8,128)(2,1)S(1)}, bf16[160,1024]{1,0:T(8,128)(2,1)S(1)}, u32[]{:S(2)}, u32[]{:S(2)}) collective-permute-start(bf16[160,1024]{1,0:T(8,128)(2,1)S(1)} %collective-permute-done.refs_2_), channel_id=1, source_target_pairs={{0,15},{1,0},{2,1},{3,2},{4,3},{5,4},{6,5},{7,6},{8,7},{9,8},{10,9... | collective-permute-start | bytes 983048 | tf_op jit(solution)/shard_map/ppermute | solution.py:79
  49.5 13.2 %collective-permute-start.1 = (bf16[160,1024]{1,0:T(8,128)(2,1)S(1)}, bf16[160,1024]{1,0:T(8,128)(2,1)S(1)}, u32[]{:S(2)}, u32[]{:S(2)}) collective-permute-start(bf16[160,1024]{1,0:T(8,128)(2,1)S(1)} %collective-permute-done.refs_2_), channel_id=1, source_target_pairs={{0,1},{1,2},{2,3},{3,4},{4,5},{5,6},{6,7},{7,8},{8,9},{9,10},{10,1... | collective-permute-start | bytes 983048 | tf_op jit(solution)/shard_map/ppermute | solution.py:79
  63.5 19.9 %collective-permute-start.6 = (bf16[320,1024]{1,0:T(8,128)(2,1)}, bf16[320,1024]{1,0:T(8,128)(2,1)S(1)}, u32[]{:S(2)}, u32[]{:S(2)}) collective-permute-start(bf16[320,1024]{1,0:T(8,128)(2,1)} %pad_maximum_fusion), channel_id=1, source_target_pairs={{0,16},{1,17},{2,18},{3,19},{4,20},{5,21},{6,22},{7,23},{8,24},{9,... | collective-permute-start | bytes 1966088 | tf_op jit(solution)/shard_map/ppermute | solution.py:79
  65.7 12.4 %collective-permute-start.4 = (bf16[160,1024]{1,0:T(8,128)(2,1)S(1)}, bf16[160,1024]{1,0:T(8,128)(2,1)}, u32[]{:S(2)}, u32[]{:S(2)}) collective-permute-start(bf16[160,1024]{1,0:T(8,128)(2,1)S(1)} %collective-permute-done.1.refs_3_), channel_id=1, source_target_pairs={{0,1},{1,2},{2,3},{3,4},{4,5},{5,6},{6,7},{7,8},{8,9},{9,10},{10,1... | collective-permute-start | bytes 983048 | tf_op jit(solution)/shard_map/ppermute | solution.py:79
  67.6 11.5 %collective-permute-start.5 = (bf16[160,1024]{1,0:T(8,128)(2,1)S(1)}, bf16[160,1024]{1,0:T(8,128)(2,1)}, u32[]{:S(2)}, u32[]{:S(2)}) collective-permute-start(bf16[160,1024]{1,0:T(8,128)(2,1)S(1)} %collective-permute-done.2.refs_4_), channel_id=1, source_target_pairs={{0,15},{1,0},{2,1},{3,2},{4,3},{5,4},{6,5},{7,6},{8,7},{9,8},{10,9... | collective-permute-start | bytes 983048 | tf_op jit(solution)/shard_map/ppermute | solution.py:79

commit v4 on v3

--- a/solution.py
+++ b/solution.py
@@ -15,22 +15,22 @@
 LIMIT = 32 * 1024 * 1024
 
 PLACES = (
-    (9, 1, 21, 29, 2, 10, 22, 30, 14, 6, 26, 18, 5, 13, 25, 17, 12, 4, 24, 16, 0, 8, 20, 28, 7, 15, 19, 27, 3, 11, 31, 23),
-    (8, 0, 28, 20, 4, 12, 24, 16, 11, 3, 31, 23, 7, 15, 27, 19, 6, 14, 26, 18, 1, 9, 21, 29, 13, 5, 17, 25, 10, 2, 22, 30),
-    (18, 26, 14, 6, 30, 22, 10, 2, 17, 25, 5, 13, 29, 21, 1, 9, 23, 31, 11, 3, 19, 27, 15, 7, 28, 20, 0, 8, 24, 16, 12, 4),
-    (19, 27, 7, 15, 23, 31, 3, 11, 16, 24, 12, 4, 28, 20, 8, 0, 18, 26, 6, 14, 21, 29, 9, 1, 30, 22, 2, 10, 25, 17, 5, 13),
-    (13, 5, 17, 25, 9, 1, 29, 21, 2, 10, 22, 30, 14, 6, 18, 26, 12, 4, 16, 24, 8, 0, 28, 20, 11, 3, 23, 31, 15, 7, 27, 19),
-    (15, 7, 19, 27, 3, 11, 31, 23, 0, 8, 28, 20, 12, 4, 24, 16, 13, 5, 25, 17, 6, 14, 18, 26, 1, 9, 21, 29, 2, 10, 30, 22),
-    (18, 26, 14, 6, 17, 25, 5, 13, 29, 21, 1, 9, 22, 30, 10, 2, 16, 24, 4, 12, 20, 28, 8, 0, 31, 23, 3, 11, 19, 27, 15, 7),
-    (19, 27, 15, 7, 31, 23, 3, 11, 28, 20, 8, 0, 16, 24, 12, 4, 22, 30, 10, 2, 21, 29, 9, 1, 26, 18, 14, 6, 25, 17, 13, 5),
-    (22, 30, 2, 10, 21, 29, 9, 1, 26, 18, 14, 6, 17, 25, 5, 13, 27, 19, 7, 15, 31, 23, 11, 3, 24, 16, 12, 4, 28, 20, 0, 8),
-    (28, 20, 8, 0, 27, 19, 15, 7, 31, 23, 11, 3, 16, 24, 4, 12, 18, 26, 14, 6, 17, 25, 5, 13, 30, 22, 2, 10, 29, 21, 9, 1),
-    (1, 9, 29, 21, 6, 14, 26, 18, 13, 5, 17, 25, 2, 10, 30, 22, 8, 0, 20, 28, 4, 12, 24, 16, 11, 3, 31, 23, 15, 7, 27, 19),
-    (15, 7, 19, 27, 8, 0, 20, 28, 4, 12, 24, 16, 11, 3, 31, 23, 10, 2, 30, 22, 5, 13, 25, 17, 14, 6, 26, 18, 9, 1, 21, 29),
-    (21, 29, 9, 1, 18, 26, 6, 14, 25, 17, 13, 5, 22, 30, 2, 10, 24, 16, 12, 4, 23, 31, 11, 3, 27, 19, 7, 15, 20, 28, 8, 0),
-    (27, 19, 7, 15, 20, 28, 0, 8, 16, 24, 12, 4, 23, 31, 3, 11, 30, 22, 10, 2, 17, 25, 5, 13, 18, 26, 14, 6, 21, 29, 1, 9),
-    (9, 1, 29, 21, 6, 14, 26, 18, 5, 13, 17, 25, 2, 10, 22, 30, 7, 15, 27, 19, 11, 3, 23, 31, 4, 12, 24, 16, 0, 8, 20, 28),
-    (12, 4, 16, 24, 8, 0, 28, 20, 7, 15, 27, 19, 11, 3, 31, 23, 13, 5, 17, 25, 10, 2, 30, 22, 1, 9, 21, 29, 14, 6, 26, 18),
+    (6, 14, 26, 18, 9, 1, 21, 29, 5, 13, 25, 17, 2, 10, 22, 30, 12, 4, 24, 16, 0, 8, 28, 20, 3, 11, 23, 31, 15, 7, 19, 27),
+    (15, 7, 19, 27, 3, 11, 23, 31, 0, 8, 28, 20, 4, 12, 16, 24, 13, 5, 25, 17, 10, 2, 22, 30, 6, 14, 26, 18, 1, 9, 21, 29),
+    (17, 25, 13, 5, 30, 22, 2, 10, 26, 18, 14, 6, 21, 29, 1, 9, 24, 16, 4, 12, 28, 20, 0, 8, 19, 27, 15, 7, 23, 31, 3, 11),
+    (19, 27, 7, 15, 23, 31, 11, 3, 16, 24, 4, 12, 28, 20, 8, 0, 30, 22, 10, 2, 21, 29, 9, 1, 25, 17, 5, 13, 26, 18, 6, 14),
+    (2, 10, 30, 22, 1, 9, 29, 21, 5, 13, 25, 17, 6, 14, 26, 18, 4, 12, 16, 24, 8, 0, 20, 28, 11, 3, 23, 31, 15, 7, 27, 19),
+    (15, 7, 27, 19, 11, 3, 23, 31, 0, 8, 20, 28, 4, 12, 16, 24, 13, 5, 25, 17, 2, 10, 30, 22, 14, 6, 26, 18, 1, 9, 29, 21),
+    (18, 26, 14, 6, 22, 30, 10, 2, 17, 25, 13, 5, 29, 21, 1, 9, 16, 24, 12, 4, 28, 20, 0, 8, 31, 23, 3, 11, 27, 19, 15, 7),
+    (19, 27, 15, 7, 31, 23, 11, 3, 28, 20, 8, 0, 24, 16, 12, 4, 17, 25, 13, 5, 21, 29, 1, 9, 26, 18, 14, 6, 22, 30, 2, 10),
+    (18, 26, 14, 6, 29, 21, 1, 9, 22, 30, 10, 2, 25, 17, 5, 13, 31, 23, 11, 3, 19, 27, 7, 15, 16, 24, 12, 4, 20, 28, 0, 8),
+    (28, 20, 8, 0, 24, 16, 12, 4, 19, 27, 7, 15, 23, 31, 11, 3, 30, 22, 10, 2, 17, 25, 5, 13, 29, 21, 1, 9, 18, 26, 6, 14),
+    (1, 9, 29, 21, 6, 14, 18, 26, 2, 10, 22, 30, 13, 5, 25, 17, 0, 8, 20, 28, 4, 12, 24, 16, 7, 15, 19, 27, 3, 11, 31, 23),
+    (3, 11, 23, 31, 15, 7, 19, 27, 4, 12, 24, 16, 0, 8, 28, 20, 5, 13, 17, 25, 2, 10, 30, 22, 9, 1, 29, 21, 14, 6, 26, 18),
+    (17, 25, 13, 5, 29, 21, 9, 1, 30, 22, 2, 10, 18, 26, 14, 6, 28, 20, 0, 8, 24, 16, 4, 12, 19, 27, 15, 7, 23, 31, 11, 3),
+    (31, 23, 11, 3, 27, 19, 7, 15, 16, 24, 12, 4, 28, 20, 0, 8, 26, 18, 14, 6, 22, 30, 2, 10, 21, 29, 9, 1, 25, 17, 5, 13),
+    (14, 6, 26, 18, 9, 1, 29, 21, 2, 10, 22, 30, 13, 5, 25, 17, 0, 8, 20, 28, 4, 12, 24, 16, 15, 7, 27, 19, 11, 3, 31, 23),
+    (11, 3, 31, 23, 15, 7, 19, 27, 12, 4, 24, 16, 8, 0, 28, 20, 13, 5, 25, 17, 10, 2, 30, 22, 9, 1, 21, 29, 14, 6, 26, 18),
 )
 
 
@@ -124,6 +124,23 @@
         compiler_params=pltpu.CompilerParams(vmem_limit_bytes=LIMIT),
         cost_estimate=pl.CostEstimate(flops=COLS, bytes_accessed=COLS, transcendentals=0),
     )(weights, rows)
+
+
+def stack_body(first, second, out):
+    out[:ROWS, :] = first[...]
+    out[ROWS:, :] = second[...]
+
+
+def stack(first, second):
+    whole = pl.BlockSpec(memory_space=pltpu.VMEM)
+    return pl.pallas_call(
+        stack_body,
+        out_shape=jax.ShapeDtypeStruct((2 * ROWS, DEPTH), jnp.bfloat16),
+        in_specs=[whole, whole],
+        out_specs=whole,
+        compiler_params=pltpu.CompilerParams(vmem_limit_bytes=LIMIT),
+        cost_estimate=pl.CostEstimate(flops=ROWS, bytes_accessed=ROWS, transcendentals=0),
+    )(first, second)
 
 
 def multiply_body(first, order, columns, *rest):
@@ -195,13 +212,14 @@
     steps = jnp.array([0, 7, 1, 4, 6, 2, 3, 5], jnp.int32)
     order = jnp.take(jnp.asarray(chunk_table()), row * CHUNKS + (color_of(row, col) + steps) % CHUNKS)
     down, up, over, order = lax.optimization_barrier((down, up, over, order))
-    sides = jnp.concatenate([down, up], axis=0)
+    sides = stack(down, up)
     over_sides = send(sides, shift(dy=2))
     down_two = send(down, shift(dz=1))
     up_two = send(up, shift(dz=-1))
 
     response = multiply(0, order, columns, [placed, down, up, over], None)
-    response = multiply(4, order, columns, [down_two, up_two, over_sides], response)
+    response = multiply(4, order, columns, [down_two, up_two], response)
+    response = multiply(6, order, columns, [over_sides], response)
     return response.reshape(CHUNKS * ROWS, COLS)
 
 

time: 87 us -> 83.5 us (0.960)
  the two profiles are of different devices: /device:TPU:2 before, /device:TPU:25 now
where the time goes in v4:
time: 83.5 us; the launch traced here: 82.9 us
  starting transfers between devices  43.8 us (52%)
  waiting for transfers between devices  18.4 us (22%)
  Pallas kernels  7.87 us (9%)
  blocking collectives  6.48 us (8%)
  local copies, waits for them, and re-layouts  6.16 us (7%)
    ppermute x7, starting transfers between devices, send(): return lax.ppermute(block, JOINT, pairs)  39.4 us
    ppermute x7, waiting for transfers between devices, send(): return lax.ppermute(block, JOINT, pairs)  18.4 us
    pallas_call x3, Pallas kernels, multiply(): pl.pallas_call(body, out_shape=jax.ShapeDtypeStruct((CHUNKS, ROWS, COLS),...  7.14 us
    all_gather x1, blocking collectives, per_device(): lax.all_gather(own, 'prow', axis=0, tiled=True, axis_index_groups=same_x)  6.48 us
    all_to_all x1, starting transfers between devices, per_device(): lax.all_to_all(jnp.broadcast_to(group, (NX, *group.shape)), 'prow', 0, 0,...  4.42 us
    unnamed x20, local copies, waits for them, and re-layouts  4.3 us
  transfers between devices with their start and end apart: 8, of which 6 were waited for; matrix products, arithmetic and copies ran while one was open for 2% of the time, Pallas kernels for 7%

profile of v4, /device:TPU:25, one launch (start us, length us, event | category | flops | bytes accessed | tf_op | source)
XLA Modules:
  0.0 82.9 jit_solution(260949729113218807)
XLA Ops:
  0.0 0.9 %copy-done.4 = bf16[40,1024]{1,0:T(8,128)(2,1)S(1)} copy-done((bf16[40,1024]{1,0:T(8,128)(2,1)S(1)}, bf16[40,1024]{1,0:T(8,128)(2,1)}, u32[]{:S(2)}) %copy-start.4) | copy-done | bytes 81944
  0.9 0.7 copy-done.5
  1.6 0.3 shard_map.64
  1.9 0.0 copy-start.7
  1.9 0.0 copy-start.8
  1.9 6.5 %all_gather.3 = bf16[160,1024]{1,0:T(8,128)(2,1)S(1)} all-gather(bf16[40,1024]{1,0:T(8,128)(2,1)S(1)} %shard_map.64), channel_id=1, replica_groups={{0,32,64,96},{128,160,192,224},{256,288,320,352},{384,416,448,480},{1,3..., dimensions={0}, use_global_device_ids=true | all-gather | bytes 409600 | tf_op jit(solution)/shard_map/all_gather | solution.py:200
  8.4 13.9 %collective-permute-start = (bf16[160,1024]{1,0:T(8,128)(2,1)S(1)}, bf16[160,1024]{1,0:T(8,128)(2,1)S(1)}, u32[]{:S(2)}, u32[]{:S(2)}) collective-permute-start(bf16[160,1024]{1,0:T(8,128)(2,1)S(1)} %all_gather.3), channel_id=1, source_target_pairs={{0,6},{1,12},{2,47},{3,45},{4,81},{5,88},{6,115},{7,126},{8,130},{... | collective-permute-start | bytes 983048 | tf_op jit(solution)/shard_map/ppermute | solution.py:79
  22.3 1.2 %broadcast_in_dim.12 = bf16[4,160,1024]{2,1,0:T(8,128)(2,1)} broadcast(bf16[160,1024]{1,0:T(8,128)(2,1)S(1)} %all_gather.3), dimensions={1,2} | broadcast | bytes 1638400 | tf_op jit(solution)/shard_map/broadcast_in_dim | solution.py:205
  23.5 4.4 %all-to-all-start = ((bf16[4,160,1024]{2,1,0:T(8,128)(2,1)}), bf16[4,160,1024]{2,1,0:T(8,128)(2,1)S(1)}, u32[]{:S(2)}, u32[]{:S(2)}) async-start(bf16[4,160,1024]{2,1,0:T(8,128)(2,1)} %broadcast_in_dim.12), calls=%async_computation | async-start | bytes 2621440 | tf_op jit(solution)/shard_map/all_to_all | solution.py:204
  28.0 0.0 copy-done.9
  28.0 4.3 %collective-permute-done.refs_2_ = bf16[160,1024]{1,0:T(8,128)(2,1)S(1)} collective-permute-done((bf16[160,1024]{1,0:T(8,128)(2,1)S(1)}, bf16[160,1024]{1,0:T(8,128)(2,1)S(1)}, u32[]{:S(2)}, u32[]{:S(2)}) %collective-permute-start) | collective-permute-done | bytes 327712 | tf_op jit(solution)/shard_map/ppermute | solution.py:79
  32.2 9.8 %collective-permute-start.3 = (bf16[160,1024]{1,0:T(8,128)(2,1)S(1)}, bf16[160,1024]{1,0:T(8,128)(2,1)S(1)}, u32[]{:S(2)}, u32[]{:S(2)}) collective-permute-start(bf16[160,1024]{1,0:T(8,128)(2,1)S(1)} %collective-permute-done.refs_2_), channel_id=1, source_target_pairs={{0,16},{1,17},{2,18},{3,19},{4,20},{5,21},{6,22},{7,23},{8,24},{9,... | collective-permute-start | bytes 983048 | tf_op jit(solution)/shard_map/ppermute | solution.py:79
  42.0 4.1 %collective-permute-start.2 = (bf16[160,1024]{1,0:T(8,128)(2,1)S(1)}, bf16[160,1024]{1,0:T(8,128)(2,1)S(1)}, u32[]{:S(2)}, u32[]{:S(2)}) collective-permute-start(bf16[160,1024]{1,0:T(8,128)(2,1)S(1)} %collective-permute-done.refs_2_), channel_id=1, source_target_pairs={{0,15},{1,0},{2,1},{3,2},{4,3},{5,4},{6,5},{7,6},{8,7},{9,8},{10,9... | collective-permute-start | bytes 983048 | tf_op jit(solution)/shard_map/ppermute | solution.py:79
  46.2 1.9 %collective-permute-start.1 = (bf16[160,1024]{1,0:T(8,128)(2,1)S(1)}, bf16[160,1024]{1,0:T(8,128)(2,1)S(1)}, u32[]{:S(2)}, u32[]{:S(2)}) collective-permute-start(bf16[160,1024]{1,0:T(8,128)(2,1)S(1)} %collective-permute-done.refs_2_), channel_id=1, source_target_pairs={{0,1},{1,2},{2,3},{3,4},{4,5},{5,6},{6,7},{7,8},{8,9},{9,10},{10,1... | collective-permute-start | bytes 983048 | tf_op jit(solution)/shard_map/ppermute | solution.py:79
  48.1 0.6 gather_fusion
  48.8 1.0 %collective-permute-done.3.refs_5_ = bf16[160,1024]{1,0:T(8,128)(2,1)S(1)} collective-permute-done((bf16[160,1024]{1,0:T(8,128)(2,1)S(1)}, bf16[160,1024]{1,0:T(8,128)(2,1)S(1)}, u32[]{:S(2)}, u32[]{:S(2)}) %collective-permute-start.3) | collective-permute-done | bytes 327712 | tf_op jit(solution)/shard_map/ppermute | solution.py:79
  49.8 0.7 copy-done.2
  50.6 2.0 %collective-permute-done.2.second.refs_4_ = bf16[160,1024]{1,0:T(8,128)(2,1)S(1)} collective-permute-done((bf16[160,1024]{1,0:T(8,128)(2,1)S(1)}, bf16[160,1024]{1,0:T(8,128)(2,1)S(1)}, u32[]{:S(2)}, u32[]{:S(2)}) %collective-permute-start.2) | collective-permute-done | bytes 327712 | tf_op jit(solution)/shard_map/ppermute | solution.py:79
  52.5 9.2 %collective-permute-done.1.first.refs_3_ = bf16[160,1024]{1,0:T(8,128)(2,1)S(1)} collective-permute-done((bf16[160,1024]{1,0:T(8,128)(2,1)S(1)}, bf16[160,1024]{1,0:T(8,128)(2,1)S(1)}, u32[]{:S(2)}, u32[]{:S(2)}) %collective-permute-start.1) | collective-permute-done | bytes 327712 | tf_op jit(solution)/shard_map/ppermute | solution.py:79
  61.8 3.1 %collective-permute-start.4 = (bf16[320,1024]{1,0:T(8,128)(2,1)S(1)}, bf16[320,1024]{1,0:T(8,128)(2,1)S(1)}, u32[]{:S(2)}, u32[]{:S(2)}) collective-permute-start(bf16[320,1024]{1,0:T(8,128)(2,1)S(1)} %shard_map.66), channel_id=1, source_target_pairs={{0,16},{1,17},{2,18},{3,19},{4,20},{5,21},{6,22},{7,23},{8,24},{9,... | collective-permute-start | bytes 1966088 | tf_op jit(solution)/shard_map/ppermute | solution.py:79
  65.0 1.9 %collective-permute-start.5 = (bf16[160,1024]{1,0:T(8,128)(2,1)S(1)}, bf16[160,1024]{1,0:T(8,128)(2,1)}, u32[]{:S(2)}, u32[]{:S(2)}) collective-permute-start(bf16[160,1024]{1,0:T(8,128)(2,1)S(1)} %collective-permute-done.1.first.refs_3_), channel_id=1, source_target_pairs={{0,1},{1,2},{2,3},{3,4},{4,5},{5,6},{6,7},{7,8},{8,9},{9,10},{10,1... | collective-permute-start | bytes 983048 | tf_op jit(solution)/shard_map/ppermute | solution.py:79
  66.9 4.6 %collective-permute-start.6 = (bf16[160,1024]{1,0:T(8,128)(2,1)S(1)}, bf16[160,1024]{1,0:T(8,128)(2,1)}, u32[]{:S(2)}, u32[]{:S(2)}) collective-permute-start(bf16[160,1024]{1,0:T(8,128)(2,1)S(1)} %collective-permute-done.2.second.refs_4_), channel_id=1, source_target_pairs={{0,15},{1,0},{2,1},{3,2},{4,3},{5,4},{6,5},{7,6},{8,7},{9,8},{10,9... | collective-permute-start | bytes 983048 | tf_op jit(solution)/shard_map/ppermute | solution.py:79
  71.5 0.0 all-to-all-done
  71.5 0.4 shard_map.65.refs_1_
  71.9 1.0 %copy-done.1 = bf16[160,1024]{1,0:T(8,128)(2,1)S(1)} copy-done((bf16[160,1024]{1,0:T(8,128)(2,1)S(1)}, bf16[160,1024]{1,0:T(8,128)(2,1)}, u32[]{:S(2)}) %copy-start.1) | copy-done | bytes 327704
  72.9 1.0 %copy-done.3 = bf16[160,1024]{1,0:T(8,128)(2,1)S(1)} copy-done((bf16[160,1024]{1,0:T(8,128)(2,1)S(1)}, bf16[160,1024]{1,0:T(8,128)(2,1)}, u32[]{:S(2)}) %copy-start.3) | copy-done | bytes 327704
  73.9 2.5 %shard_map.67.refs_4_ = f32[8,160,640]{2,1,0:T(8,128)} custom-call(s32[8]{0:T(128)S(1)} %and_select_fusion.refs_0_, bf16[1024,640]{1,0:T(8,128)(2,1)S(1)} %shard_map.65.refs_1_, bf16[160,1024]{1,0:T(8,128)(2,1)S(1)} %copy-done.1, bf16[160,1024]{1,0:T(8,128)(2,1)S(1)} %collective-permute-done.1.first.refs_3_, ...), custom_call_target="tpu_custom_call" | custom-call | flops 640 | bytes 640 | tf_op jit(solution)/shard_map/pallas_call | solution.py:178
  76.4 0.4 collective-permute-done.5.refs_2_
  76.8 1.5 %collective-permute-done.6.refs_3_ = bf16[160,1024]{1,0:T(8,128)(2,1)} collective-permute-done((bf16[160,1024]{1,0:T(8,128)(2,1)S(1)}, bf16[160,1024]{1,0:T(8,128)(2,1)}, u32[]{:S(2)}, u32[]{:S(2)}) %collective-permute-start.6) | collective-permute-done | bytes 327712 | tf_op jit(solution)/shard_map/ppermute | solution.py:79
  78.3 2.6 %shard_map.68.refs_3_ = f32[8,160,640]{2,1,0:T(8,128)} custom-call(s32[8]{0:T(128)S(1)} %and_select_fusion.refs_0_, bf16[1024,640]{1,0:T(8,128)(2,1)S(1)} %shard_map.65.refs_1_, bf16[160,1024]{1,0:T(8,128)(2,1)} %collective-permute-done.5.refs_2_, bf16[160,1024]{1,0:T(8,128)(2,1)} %collective-permute-done.6.refs_3_, ...), custom_call_target="tpu_custom_call", output_to_operand_aliasing={{}: (4, {})} | custom-call | flops 320 | bytes 320 | tf_op jit(solution)/shard_map/pallas_call | solution.py:178
  80.9 0.0 collective-permute-done.4.refs_2_
  80.9 2.0 %shard_map.69 = f32[8,160,640]{2,1,0:T(8,128)} custom-call(s32[8]{0:T(128)S(1)} %and_select_fusion.refs_0_, bf16[1024,640]{1,0:T(8,128)(2,1)S(1)} %shard_map.65.refs_1_, bf16[320,1024]{1,0:T(8,128)(2,1)S(1)} %collective-permute-done.4.refs_2_, f32[8,160,640]{2,1,0:T(8,128)} %shard_map.68.refs_3_), custom_call_target="tpu_custom_call", output_to_operand_aliasing={{}: (3, {})} | custom-call | flops 320 | bytes 320 | tf_op jit(solution)/shard_map/pallas_call | solution.py:178
  (17 shorter events, 0.1 us)
Async XLA Ops:
  0.0 28.0 %copy-start.9 = (s32[8]{0:T(128)S(1)}, s32[8]{0:T(128)}, u32[]{:S(2)}) copy-start(s32[8]{0:T(128)} %constant.82.clone) | copy-start | bytes 100
  0.0 48.1 %copy-start.6 = (s32[128]{0:T(128)S(1)}, s32[128]{0:T(128)}, u32[]{:S(2)}) copy-start(s32[128]{0:T(128)} %constant.86) | copy-start | bytes 1540
  0.0 0.9 %copy-start.4 = (bf16[40,1024]{1,0:T(8,128)(2,1)S(1)}, bf16[40,1024]{1,0:T(8,128)(2,1)}, u32[]{:S(2)}) copy-start(bf16[40,1024]{1,0:T(8,128)(2,1)} %mantissa_ref.1) | copy-start | bytes 245764
  0.9 0.7 copy-start.5
  1.9 69.6 %copy-start.7 = (s32[1024]{0:T(1024)S(1)}, s32[1024]{0:T(1024)}, u32[]{:S(2)}) copy-start(s32[1024]{0:T(1024)} %param.9) | copy-start | bytes 12292
  1.9 69.6 %copy-start.8 = (s32[1024]{0:T(1024)S(1)}, s32[1024]{0:T(1024)}, u32[]{:S(2)}) copy-start(s32[1024]{0:T(1024)} %param.8) | copy-start | bytes 12292
  8.4 23.8 %collective-permute-start = (bf16[160,1024]{1,0:T(8,128)(2,1)S(1)}, bf16[160,1024]{1,0:T(8,128)(2,1)S(1)}, u32[]{:S(2)}, u32[]{:S(2)}) collective-permute-start(bf16[160,1024]{1,0:T(8,128)(2,1)S(1)} %all_gather.3), channel_id=1, source_target_pairs={{0,6},{1,12},{2,47},{3,45},{4,81},{5,88},{6,115},{7,126},{8,130},{... | collective-permute-start | bytes 983048 | tf_op jit(solution)/shard_map/ppermute | solution.py:79
  23.5 48.0 %all-to-all-start = ((bf16[4,160,1024]{2,1,0:T(8,128)(2,1)}), bf16[4,160,1024]{2,1,0:T(8,128)(2,1)S(1)}, u32[]{:S(2)}, u32[]{:S(2)}) async-start(bf16[4,160,1024]{2,1,0:T(8,128)(2,1)} %broadcast_in_dim.12), calls=%async_computation | async-start | bytes 2621440 | tf_op jit(solution)/shard_map/all_to_all | solution.py:204
  32.2 29.5 %copy-start = (bf16[160,1024]{1,0:T(8,128)(2,1)}, bf16[160,1024]{1,0:T(8,128)(2,1)S(1)}, u32[]{:S(2)}) copy-start(bf16[160,1024]{1,0:T(8,128)(2,1)S(1)} %collective-permute-done.refs_2_) | copy-start | bytes 983044
  32.2 17.6 %collective-permute-start.3 = (bf16[160,1024]{1,0:T(8,128)(2,1)S(1)}, bf16[160,1024]{1,0:T(8,128)(2,1)S(1)}, u32[]{:S(2)}, u32[]{:S(2)}) collective-permute-start(bf16[160,1024]{1,0:T(8,128)(2,1)S(1)} %collective-permute-done.refs_2_), channel_id=1, source_target_pairs={{0,16},{1,17},{2,18},{3,19},{4,20},{5,21},{6,22},{7,23},{8,24},{9,... | collective-permute-start | bytes 983048 | tf_op jit(solution)/shard_map/ppermute | solution.py:79
  42.0 10.5 %collective-permute-start.2 = (bf16[160,1024]{1,0:T(8,128)(2,1)S(1)}, bf16[160,1024]{1,0:T(8,128)(2,1)S(1)}, u32[]{:S(2)}, u32[]{:S(2)}) collective-permute-start(bf16[160,1024]{1,0:T(8,128)(2,1)S(1)} %collective-permute-done.refs_2_), channel_id=1, source_target_pairs={{0,15},{1,0},{2,1},{3,2},{4,3},{5,4},{6,5},{7,6},{8,7},{9,8},{10,9... | collective-permute-start | bytes 983048 | tf_op jit(solution)/shard_map/ppermute | solution.py:79
  46.2 15.6 %collective-permute-start.1 = (bf16[160,1024]{1,0:T(8,128)(2,1)S(1)}, bf16[160,1024]{1,0:T(8,128)(2,1)S(1)}, u32[]{:S(2)}, u32[]{:S(2)}) collective-permute-start(bf16[160,1024]{1,0:T(8,128)(2,1)S(1)} %collective-permute-done.refs_2_), channel_id=1, source_target_pairs={{0,1},{1,2},{2,3},{3,4},{4,5},{5,6},{6,7},{7,8},{8,9},{9,10},{10,1... | collective-permute-start | bytes 983048 | tf_op jit(solution)/shard_map/ppermute | solution.py:79
  49.8 0.7 copy-start.2
  61.8 19.1 %collective-permute-start.4 = (bf16[320,1024]{1,0:T(8,128)(2,1)S(1)}, bf16[320,1024]{1,0:T(8,128)(2,1)S(1)}, u32[]{:S(2)}, u32[]{:S(2)}) collective-permute-start(bf16[320,1024]{1,0:T(8,128)(2,1)S(1)} %shard_map.66), channel_id=1, source_target_pairs={{0,16},{1,17},{2,18},{3,19},{4,20},{5,21},{6,22},{7,23},{8,24},{9,... | collective-permute-start | bytes 1966088 | tf_op jit(solution)/shard_map/ppermute | solution.py:79
  65.0 11.8 %collective-permute-start.5 = (bf16[160,1024]{1,0:T(8,128)(2,1)S(1)}, bf16[160,1024]{1,0:T(8,128)(2,1)}, u32[]{:S(2)}, u32[]{:S(2)}) collective-permute-start(bf16[160,1024]{1,0:T(8,128)(2,1)S(1)} %collective-permute-done.1.first.refs_3_), channel_id=1, source_target_pairs={{0,1},{1,2},{2,3},{3,4},{4,5},{5,6},{6,7},{7,8},{8,9},{9,10},{10,1... | collective-permute-start | bytes 983048 | tf_op jit(solution)/shard_map/ppermute | solution.py:79
  66.9 11.4 %collective-permute-start.6 = (bf16[160,1024]{1,0:T(8,128)(2,1)S(1)}, bf16[160,1024]{1,0:T(8,128)(2,1)}, u32[]{:S(2)}, u32[]{:S(2)}) collective-permute-start(bf16[160,1024]{1,0:T(8,128)(2,1)S(1)} %collective-permute-done.2.second.refs_4_), channel_id=1, source_target_pairs={{0,15},{1,0},{2,1},{3,2},{4,3},{5,4},{6,5},{7,6},{8,7},{9,8},{10,9... | collective-permute-start | bytes 983048 | tf_op jit(solution)/shard_map/ppermute | solution.py:79
  71.9 1.0 %copy-start.1 = (bf16[160,1024]{1,0:T(8,128)(2,1)S(1)}, bf16[160,1024]{1,0:T(8,128)(2,1)}, u32[]{:S(2)}) copy-start(bf16[160,1024]{1,0:T(8,128)(2,1)} %copy-done) | copy-start | bytes 983044
  72.9 1.0 %copy-start.3 = (bf16[160,1024]{1,0:T(8,128)(2,1)S(1)}, bf16[160,1024]{1,0:T(8,128)(2,1)}, u32[]{:S(2)}) copy-start(bf16[160,1024]{1,0:T(8,128)(2,1)} %copy-done.2) | copy-start | bytes 983044

commit v5 on v4

--- a/solution.py
+++ b/solution.py
@@ -126,23 +126,6 @@
     )(weights, rows)
 
 
-def stack_body(first, second, out):
-    out[:ROWS, :] = first[...]
-    out[ROWS:, :] = second[...]
-
-
-def stack(first, second):
-    whole = pl.BlockSpec(memory_space=pltpu.VMEM)
-    return pl.pallas_call(
-        stack_body,
-        out_shape=jax.ShapeDtypeStruct((2 * ROWS, DEPTH), jnp.bfloat16),
-        in_specs=[whole, whole],
-        out_specs=whole,
-        compiler_params=pltpu.CompilerParams(vmem_limit_bytes=LIMIT),
-        cost_estimate=pl.CostEstimate(flops=ROWS, bytes_accessed=ROWS, transcendentals=0),
-    )(first, second)
-
-
 def multiply_body(first, order, columns, *rest):
     *blocks, response, held, sems = rest
     copies = []
@@ -209,17 +192,17 @@
     over = send(placed, shift(dy=2))
     weights = pair_weights(occ_level, virt_level)[None, :]
     columns = scale(weights, groups.reshape(COLS, DEPTH))
-    steps = jnp.array([0, 7, 1, 4, 6, 2, 3, 5], jnp.int32)
+    steps = jnp.array([0, 1, 4, 7, 2, 5, 6, 3], jnp.int32)
     order = jnp.take(jnp.asarray(chunk_table()), row * CHUNKS + (color_of(row, col) + steps) % CHUNKS)
-    down, up, over, order = lax.optimization_barrier((down, up, over, order))
-    sides = stack(down, up)
-    over_sides = send(sides, shift(dy=2))
+    over_up = send(up, shift(dy=2))
+    over_down = send(down, shift(dy=2))
+    up_two = send(up, shift(dz=-1))
     down_two = send(down, shift(dz=1))
-    up_two = send(up, shift(dz=-1))
-
-    response = multiply(0, order, columns, [placed, down, up, over], None)
-    response = multiply(4, order, columns, [down_two, up_two], response)
-    response = multiply(6, order, columns, [over_sides], response)
+
+    response = multiply(0, order, columns, [placed, up, over], None)
+    response = multiply(3, order, columns, [down], response)
+    response = multiply(4, order, columns, [up_two, over_up], response)
+    response = multiply(6, order, columns, [down_two, over_down], response)
     return response.reshape(CHUNKS * ROWS, COLS)
 
 

time: 83.5 us -> 81.2 us (0.972)
  waiting for transfers between devices: 18.4 us -> 8.98 us
  starting transfers between devices: 43.8 us -> 51.8 us
  local copies, waits for them, and re-layouts: 6.16 us -> 3.48 us
  Pallas kernels: 7.87 us -> 9.63 us
    ppermute x7 -> x8, waiting for transfers between devices: 18.4 us -> 8.98 us  [send(): return lax.ppermute(block, JOINT, pairs)]
    ppermute x7 -> x8, starting transfers between devices: 39.4 us -> 47.4 us  [send(): return lax.ppermute(block, JOINT, pairs)]
    unnamed x20 -> x12, local copies, waits for them, and re-layouts: 4.3 us -> 1.61 us
    pallas_call x3 -> x4, Pallas kernels: 7.14 us -> 8.92 us  [multiply(): pl.pallas_call(body, out_shape=jax.ShapeDtypeStruct((CHUNKS, ROWS, COLS),...]
  transfers between devices with their start and end apart: 8 -> 9, of which waited for: 6 -> 3; matrix products, arithmetic and copies ran while one was open for 2% -> 2% of each run, Pallas kernels for 7% -> 9%
where the time goes in v5:
time: 81.2 us; the launch traced here: 80.6 us
  starting transfers between devices  51.8 us (64%)
  Pallas kernels  9.63 us (12%)
  waiting for transfers between devices  8.98 us (11%)
  blocking collectives  6.48 us (8%)
  local copies, waits for them, and re-layouts  3.48 us (4%)
    ppermute x8, starting transfers between devices, send(): return lax.ppermute(block, JOINT, pairs)  47.4 us
    ppermute x8, waiting for transfers between devices, send(): return lax.ppermute(block, JOINT, pairs)  8.98 us
    pallas_call x4, Pallas kernels, multiply(): pl.pallas_call(body, out_shape=jax.ShapeDtypeStruct((CHUNKS, ROWS, COLS),...  8.92 us
    all_gather x1, blocking collectives, per_device(): lax.all_gather(own, 'prow', axis=0, tiled=True, axis_index_groups=same_x)  6.48 us
    all_to_all x1, starting transfers between devices, per_device(): lax.all_to_all(jnp.broadcast_to(group, (NX, *group.shape)), 'prow', 0, 0,...  4.42 us
  transfers between devices with their start and end apart: 9, of which 3 were waited for; matrix products, arithmetic and copies ran while one was open for 2% of the time, Pallas kernels for 9%

profile of v5, /device:TPU:25, one launch (start us, length us, event | category | flops | bytes accessed | tf_op | source)
XLA Modules:
  0.0 80.6 jit_solution(14285662239816182557)
XLA Ops:
  0.0 0.9 %copy-done = bf16[40,1024]{1,0:T(8,128)(2,1)S(1)} copy-done((bf16[40,1024]{1,0:T(8,128)(2,1)S(1)}, bf16[40,1024]{1,0:T(8,128)(2,1)}, u32[]{:S(2)}) %copy-start) | copy-done | bytes 81944
  0.9 0.7 copy-done.1
  1.6 0.3 shard_map.64
  1.9 6.5 %all_gather.3 = bf16[160,1024]{1,0:T(8,128)(2,1)S(1)} all-gather(bf16[40,1024]{1,0:T(8,128)(2,1)S(1)} %shard_map.64), channel_id=1, replica_groups={{0,32,64,96},{128,160,192,224},{256,288,320,352},{384,416,448,480},{1,3..., dimensions={0}, use_global_device_ids=true | all-gather | bytes 409600 | tf_op jit(solution)/shard_map/all_gather | solution.py:183
  8.4 13.9 %collective-permute-start = (bf16[160,1024]{1,0:T(8,128)(2,1)S(1)}, bf16[160,1024]{1,0:T(8,128)(2,1)S(1)}, u32[]{:S(2)}, u32[]{:S(2)}) collective-permute-start(bf16[160,1024]{1,0:T(8,128)(2,1)S(1)} %all_gather.3), channel_id=1, source_target_pairs={{0,6},{1,12},{2,47},{3,45},{4,81},{5,88},{6,115},{7,126},{8,130},{... | collective-permute-start | bytes 983048 | tf_op jit(solution)/shard_map/ppermute | solution.py:79
  22.3 1.2 %broadcast_in_dim.12 = bf16[4,160,1024]{2,1,0:T(8,128)(2,1)} broadcast(bf16[160,1024]{1,0:T(8,128)(2,1)S(1)} %all_gather.3), dimensions={1,2} | broadcast | bytes 1638400 | tf_op jit(solution)/shard_map/broadcast_in_dim | solution.py:188
  23.5 4.4 %all-to-all-start = ((bf16[4,160,1024]{2,1,0:T(8,128)(2,1)}), bf16[4,160,1024]{2,1,0:T(8,128)(2,1)S(1)}, u32[]{:S(2)}, u32[]{:S(2)}) async-start(bf16[4,160,1024]{2,1,0:T(8,128)(2,1)} %broadcast_in_dim.12), calls=%async_computation | async-start | bytes 2621440 | tf_op jit(solution)/shard_map/all_to_all | solution.py:187
  28.0 4.3 %collective-permute-done.refs_2_ = bf16[160,1024]{1,0:T(8,128)(2,1)S(1)} collective-permute-done((bf16[160,1024]{1,0:T(8,128)(2,1)S(1)}, bf16[160,1024]{1,0:T(8,128)(2,1)S(1)}, u32[]{:S(2)}, u32[]{:S(2)}) %collective-permute-start) | collective-permute-done | bytes 327712 | tf_op jit(solution)/shard_map/ppermute | solution.py:79
  32.2 12.0 %collective-permute-start.4 = (bf16[160,1024]{1,0:T(8,128)(2,1)S(1)}, bf16[160,1024]{1,0:T(8,128)(2,1)S(1)}, u32[]{:S(2)}, u32[]{:S(2)}) collective-permute-start(bf16[160,1024]{1,0:T(8,128)(2,1)S(1)} %collective-permute-done.refs_2_), channel_id=1, source_target_pairs={{0,15},{1,0},{2,1},{3,2},{4,3},{5,4},{6,5},{7,6},{8,7},{9,8},{10,9... | collective-permute-start | bytes 983048 | tf_op jit(solution)/shard_map/ppermute | solution.py:79
  44.2 1.9 %collective-permute-start.1 = (bf16[160,1024]{1,0:T(8,128)(2,1)S(1)}, bf16[160,1024]{1,0:T(8,128)(2,1)S(1)}, u32[]{:S(2)}, u32[]{:S(2)}) collective-permute-start(bf16[160,1024]{1,0:T(8,128)(2,1)S(1)} %collective-permute-done.refs_2_), channel_id=1, source_target_pairs={{0,1},{1,2},{2,3},{3,4},{4,5},{5,6},{6,7},{7,8},{8,9},{9,10},{10,1... | collective-permute-start | bytes 983048 | tf_op jit(solution)/shard_map/ppermute | solution.py:79
  46.2 0.0 copy-done.5
  46.2 0.0 copy-done.2
  46.2 0.6 gather_fusion
  46.9 1.9 %collective-permute-start.7 = (bf16[160,1024]{1,0:T(8,128)(2,1)S(1)}, bf16[160,1024]{1,0:T(8,128)(2,1)}, u32[]{:S(2)}, u32[]{:S(2)}) collective-permute-start(bf16[160,1024]{1,0:T(8,128)(2,1)S(1)} %collective-permute-done.refs_2_), channel_id=1, source_target_pairs={{0,16},{1,17},{2,18},{3,19},{4,20},{5,21},{6,22},{7,23},{8,24},{9,... | collective-permute-start | bytes 983048 | tf_op jit(solution)/shard_map/ppermute | solution.py:79
  48.8 2.2 %collective-permute-done.4.refs_3_ = bf16[160,1024]{1,0:T(8,128)(2,1)S(1)} collective-permute-done((bf16[160,1024]{1,0:T(8,128)(2,1)S(1)}, bf16[160,1024]{1,0:T(8,128)(2,1)S(1)}, u32[]{:S(2)}, u32[]{:S(2)}) %collective-permute-start.4) | collective-permute-done | bytes 327712 | tf_op jit(solution)/shard_map/ppermute | solution.py:79
  51.0 8.9 %collective-permute-start.5 = (bf16[160,1024]{1,0:T(8,128)(2,1)S(1)}, bf16[160,1024]{1,0:T(8,128)(2,1)S(1)}, u32[]{:S(2)}, u32[]{:S(2)}) collective-permute-start(bf16[160,1024]{1,0:T(8,128)(2,1)S(1)} %collective-permute-done.4.refs_3_), channel_id=1, source_target_pairs={{0,15},{1,0},{2,1},{3,2},{4,3},{5,4},{6,5},{7,6},{8,7},{9,8},{10,9... | collective-permute-start | bytes 983048 | tf_op jit(solution)/shard_map/ppermute | solution.py:79
  60.0 1.9 %collective-permute-start.6 = (bf16[160,1024]{1,0:T(8,128)(2,1)S(1)}, bf16[160,1024]{1,0:T(8,128)(2,1)S(1)}, u32[]{:S(2)}, u32[]{:S(2)}) collective-permute-start(bf16[160,1024]{1,0:T(8,128)(2,1)S(1)} %collective-permute-done.4.refs_3_), channel_id=1, source_target_pairs={{0,16},{1,17},{2,18},{3,19},{4,20},{5,21},{6,22},{7,23},{8,24},{9,... | collective-permute-start | bytes 983048 | tf_op jit(solution)/shard_map/ppermute | solution.py:79
  61.9 0.0 collective-permute-done.1.refs_2_
  61.9 1.9 %collective-permute-start.2 = (bf16[160,1024]{1,0:T(8,128)(2,1)S(1)}, bf16[160,1024]{1,0:T(8,128)(2,1)S(1)}, u32[]{:S(2)}, u32[]{:S(2)}) collective-permute-start(bf16[160,1024]{1,0:T(8,128)(2,1)S(1)} %collective-permute-done.1.refs_2_), channel_id=1, source_target_pairs={{0,1},{1,2},{2,3},{3,4},{4,5},{5,6},{6,7},{7,8},{8,9},{9,10},{10,1... | collective-permute-start | bytes 983048 | tf_op jit(solution)/shard_map/ppermute | solution.py:79
  63.8 4.9 %collective-permute-start.3 = (bf16[160,1024]{1,0:T(8,128)(2,1)S(1)}, bf16[160,1024]{1,0:T(8,128)(2,1)}, u32[]{:S(2)}, u32[]{:S(2)}) collective-permute-start(bf16[160,1024]{1,0:T(8,128)(2,1)S(1)} %collective-permute-done.1.refs_2_), channel_id=1, source_target_pairs={{0,16},{1,17},{2,18},{3,19},{4,20},{5,21},{6,22},{7,23},{8,24},{9,... | collective-permute-start | bytes 983048 | tf_op jit(solution)/shard_map/ppermute | solution.py:79
  68.7 0.0 copy-done.3
  68.8 0.0 all-to-all-done
  68.8 0.4 shard_map.65.refs_1_
  69.2 0.0 collective-permute-done.7.refs_4_
  69.2 2.7 %shard_map.66.refs_3_ = f32[8,160,640]{2,1,0:T(8,128)} custom-call(s32[8]{0:T(128)S(1)} %and_select_fusion.refs_0_, bf16[1024,640]{1,0:T(8,128)(2,1)S(1)} %shard_map.65.refs_1_, bf16[160,1024]{1,0:T(8,128)(2,1)S(1)} %collective-permute-done.refs_2_, bf16[160,1024]{1,0:T(8,128)(2,1)S(1)} %collective-permute-done.4.refs_3_, ...), custom_call_target="tpu_custom_call" | custom-call | flops 480 | bytes 480 | tf_op jit(solution)/shard_map/pallas_call | solution.py:161
  71.9 1.7 %shard_map.67.refs_4_ = f32[8,160,640]{2,1,0:T(8,128)} custom-call(s32[8]{0:T(128)S(1)} %and_select_fusion.refs_0_, bf16[1024,640]{1,0:T(8,128)(2,1)S(1)} %shard_map.65.refs_1_, bf16[160,1024]{1,0:T(8,128)(2,1)S(1)} %collective-permute-done.1.refs_2_, f32[8,160,640]{2,1,0:T(8,128)} %shard_map.66.refs_3_), custom_call_target="tpu_custom_call", output_to_operand_aliasing={{}: (3, {})} | custom-call | flops 160 | bytes 160 | tf_op jit(solution)/shard_map/pallas_call | solution.py:161
  73.7 0.0 collective-permute-done.5.refs_2_
  73.7 0.0 collective-permute-done.6.refs_3_
  73.7 2.0 %shard_map.68.refs_4_ = f32[8,160,640]{2,1,0:T(8,128)} custom-call(s32[8]{0:T(128)S(1)} %and_select_fusion.refs_0_, bf16[1024,640]{1,0:T(8,128)(2,1)S(1)} %shard_map.65.refs_1_, bf16[160,1024]{1,0:T(8,128)(2,1)S(1)} %collective-permute-done.5.refs_2_, bf16[160,1024]{1,0:T(8,128)(2,1)S(1)} %collective-permute-done.6.refs_3_, ...), custom_call_target="tpu_custom_call", output_to_operand_aliasing={{}: (4, {})} | custom-call | flops 320 | bytes 320 | tf_op jit(solution)/shard_map/pallas_call | solution.py:161
  75.7 0.0 collective-permute-done.2.refs_2_
  75.7 2.4 %collective-permute-done.3.refs_3_ = bf16[160,1024]{1,0:T(8,128)(2,1)} collective-permute-done((bf16[160,1024]{1,0:T(8,128)(2,1)S(1)}, bf16[160,1024]{1,0:T(8,128)(2,1)}, u32[]{:S(2)}, u32[]{:S(2)}) %collective-permute-start.3) | collective-permute-done | bytes 327712 | tf_op jit(solution)/shard_map/ppermute | solution.py:79
  78.2 2.4 %shard_map.69 = f32[8,160,640]{2,1,0:T(8,128)} custom-call(s32[8]{0:T(128)S(1)} %and_select_fusion.refs_0_, bf16[1024,640]{1,0:T(8,128)(2,1)S(1)} %shard_map.65.refs_1_, bf16[160,1024]{1,0:T(8,128)(2,1)S(1)} %collective-permute-done.2.refs_2_, bf16[160,1024]{1,0:T(8,128)(2,1)} %collective-permute-done.3.refs_3_, ...), custom_call_target="tpu_custom_call", output_to_operand_aliasing={{}: (4, {})} | custom-call | flops 320 | bytes 320 | tf_op jit(solution)/shard_map/pallas_call | solution.py:161
  (11 shorter events, 0.1 us)
Async XLA Ops:
  0.0 46.2 %copy-start.5 = (s32[8]{0:T(128)S(1)}, s32[8]{0:T(128)}, u32[]{:S(2)}) copy-start(s32[8]{0:T(128)} %constant.82.clone) | copy-start | bytes 100
  0.0 46.2 %copy-start.2 = (s32[128]{0:T(128)S(1)}, s32[128]{0:T(128)}, u32[]{:S(2)}) copy-start(s32[128]{0:T(128)} %constant.86) | copy-start | bytes 1540
  0.0 0.9 %copy-start = (bf16[40,1024]{1,0:T(8,128)(2,1)S(1)}, bf16[40,1024]{1,0:T(8,128)(2,1)}, u32[]{:S(2)}) copy-start(bf16[40,1024]{1,0:T(8,128)(2,1)} %mantissa_ref.1) | copy-start | bytes 245764
  0.9 0.7 copy-start.1
  1.6 67.1 %copy-start.3 = (s32[1024]{0:T(1024)S(1)}, s32[1024]{0:T(1024)}, u32[]{:S(2)}) copy-start(s32[1024]{0:T(1024)} %param.9) | copy-start | bytes 12292
  1.6 67.1 %copy-start.4 = (s32[1024]{0:T(1024)S(1)}, s32[1024]{0:T(1024)}, u32[]{:S(2)}) copy-start(s32[1024]{0:T(1024)} %param.8) | copy-start | bytes 12292
  8.4 23.8 %collective-permute-start = (bf16[160,1024]{1,0:T(8,128)(2,1)S(1)}, bf16[160,1024]{1,0:T(8,128)(2,1)S(1)}, u32[]{:S(2)}, u32[]{:S(2)}) collective-permute-start(bf16[160,1024]{1,0:T(8,128)(2,1)S(1)} %all_gather.3), channel_id=1, source_target_pairs={{0,6},{1,12},{2,47},{3,45},{4,81},{5,88},{6,115},{7,126},{8,130},{... | collective-permute-start | bytes 983048 | tf_op jit(solution)/shard_map/ppermute | solution.py:79
  23.5 45.2 %all-to-all-start = ((bf16[4,160,1024]{2,1,0:T(8,128)(2,1)}), bf16[4,160,1024]{2,1,0:T(8,128)(2,1)S(1)}, u32[]{:S(2)}, u32[]{:S(2)}) async-start(bf16[4,160,1024]{2,1,0:T(8,128)(2,1)} %broadcast_in_dim.12), calls=%async_computation | async-start | bytes 2621440 | tf_op jit(solution)/shard_map/all_to_all | solution.py:187
  32.2 18.8 %collective-permute-start.4 = (bf16[160,1024]{1,0:T(8,128)(2,1)S(1)}, bf16[160,1024]{1,0:T(8,128)(2,1)S(1)}, u32[]{:S(2)}, u32[]{:S(2)}) collective-permute-start(bf16[160,1024]{1,0:T(8,128)(2,1)S(1)} %collective-permute-done.refs_2_), channel_id=1, source_target_pairs={{0,15},{1,0},{2,1},{3,2},{4,3},{5,4},{6,5},{7,6},{8,7},{9,8},{10,9... | collective-permute-start | bytes 983048 | tf_op jit(solution)/shard_map/ppermute | solution.py:79
  44.2 17.7 %collective-permute-start.1 = (bf16[160,1024]{1,0:T(8,128)(2,1)S(1)}, bf16[160,1024]{1,0:T(8,128)(2,1)S(1)}, u32[]{:S(2)}, u32[]{:S(2)}) collective-permute-start(bf16[160,1024]{1,0:T(8,128)(2,1)S(1)} %collective-permute-done.refs_2_), channel_id=1, source_target_pairs={{0,1},{1,2},{2,3},{3,4},{4,5},{5,6},{6,7},{7,8},{8,9},{9,10},{10,1... | collective-permute-start | bytes 983048 | tf_op jit(solution)/shard_map/ppermute | solution.py:79
  46.9 22.3 %collective-permute-start.7 = (bf16[160,1024]{1,0:T(8,128)(2,1)S(1)}, bf16[160,1024]{1,0:T(8,128)(2,1)}, u32[]{:S(2)}, u32[]{:S(2)}) collective-permute-start(bf16[160,1024]{1,0:T(8,128)(2,1)S(1)} %collective-permute-done.refs_2_), channel_id=1, source_target_pairs={{0,16},{1,17},{2,18},{3,19},{4,20},{5,21},{6,22},{7,23},{8,24},{9,... | collective-permute-start | bytes 983048 | tf_op jit(solution)/shard_map/ppermute | solution.py:79
  51.0 22.6 %collective-permute-start.5 = (bf16[160,1024]{1,0:T(8,128)(2,1)S(1)}, bf16[160,1024]{1,0:T(8,128)(2,1)S(1)}, u32[]{:S(2)}, u32[]{:S(2)}) collective-permute-start(bf16[160,1024]{1,0:T(8,128)(2,1)S(1)} %collective-permute-done.4.refs_3_), channel_id=1, source_target_pairs={{0,15},{1,0},{2,1},{3,2},{4,3},{5,4},{6,5},{7,6},{8,7},{9,8},{10,9... | collective-permute-start | bytes 983048 | tf_op jit(solution)/shard_map/ppermute | solution.py:79
  60.0 13.7 %collective-permute-start.6 = (bf16[160,1024]{1,0:T(8,128)(2,1)S(1)}, bf16[160,1024]{1,0:T(8,128)(2,1)S(1)}, u32[]{:S(2)}, u32[]{:S(2)}) collective-permute-start(bf16[160,1024]{1,0:T(8,128)(2,1)S(1)} %collective-permute-done.4.refs_3_), channel_id=1, source_target_pairs={{0,16},{1,17},{2,18},{3,19},{4,20},{5,21},{6,22},{7,23},{8,24},{9,... | collective-permute-start | bytes 983048 | tf_op jit(solution)/shard_map/ppermute | solution.py:79
  61.9 13.8 %collective-permute-start.2 = (bf16[160,1024]{1,0:T(8,128)(2,1)S(1)}, bf16[160,1024]{1,0:T(8,128)(2,1)S(1)}, u32[]{:S(2)}, u32[]{:S(2)}) collective-permute-start(bf16[160,1024]{1,0:T(8,128)(2,1)S(1)} %collective-permute-done.1.refs_2_), channel_id=1, source_target_pairs={{0,1},{1,2},{2,3},{3,4},{4,5},{5,6},{6,7},{7,8},{8,9},{9,10},{10,1... | collective-permute-start | bytes 983048 | tf_op jit(solution)/shard_map/ppermute | solution.py:79
  63.8 14.3 %collective-permute-start.3 = (bf16[160,1024]{1,0:T(8,128)(2,1)S(1)}, bf16[160,1024]{1,0:T(8,128)(2,1)}, u32[]{:S(2)}, u32[]{:S(2)}) collective-permute-start(bf16[160,1024]{1,0:T(8,128)(2,1)S(1)} %collective-permute-done.1.refs_2_), channel_id=1, source_target_pairs={{0,16},{1,17},{2,18},{3,19},{4,20},{5,21},{6,22},{7,23},{8,24},{9,... | collective-permute-start | bytes 983048 | tf_op jit(solution)/shard_map/ppermute | solution.py:79

commit v6 on v5

--- a/solution.py
+++ b/solution.py
@@ -202,7 +202,8 @@
     response = multiply(0, order, columns, [placed, up, over], None)
     response = multiply(3, order, columns, [down], response)
     response = multiply(4, order, columns, [up_two, over_up], response)
-    response = multiply(6, order, columns, [down_two, over_down], response)
+    response = multiply(6, order, columns, [down_two], response)
+    response = multiply(7, order, columns, [over_down], response)
     return response.reshape(CHUNKS * ROWS, COLS)
 
 

time: 81.2 us -> 81.1 us (level)
  the two profiles are of different devices: /device:TPU:25 before, /device:TPU:2 now
where the time goes in v6:
time: 81.1 us; the launch traced here: 80.5 us
  starting transfers between devices  48.7 us (60%)
  Pallas kernels  11.1 us (14%)
  waiting for transfers between devices  10.7 us (13%)
  blocking collectives  6.19 us (8%)
  local copies, waits for them, and re-layouts  3.48 us (4%)
    ppermute x8, starting transfers between devices, send(): return lax.ppermute(block, JOINT, pairs)  45.2 us
    ppermute x8, waiting for transfers between devices, send(): return lax.ppermute(block, JOINT, pairs)  10.7 us
    pallas_call x5, Pallas kernels, multiply(): pl.pallas_call(body, out_shape=jax.ShapeDtypeStruct((CHUNKS, ROWS, COLS),...  10.4 us
    all_gather x1, blocking collectives, per_device(): lax.all_gather(own, 'prow', axis=0, tiled=True, axis_index_groups=same_x)  6.19 us
    all_to_all x1, starting transfers between devices, per_device(): lax.all_to_all(jnp.broadcast_to(group, (NX, *group.shape)), 'prow', 0, 0,...  3.53 us
  transfers between devices with their start and end apart: 9, of which 1 were waited for; matrix products, arithmetic and copies ran while one was open for 2% of the time, Pallas kernels for 11%

profile of v6, /device:TPU:2, one launch (start us, length us, event | category | flops | bytes accessed | tf_op | source)
XLA Modules:
  0.0 80.5 jit_solution(5229573239055604328)
XLA Ops:
  0.0 0.9 %copy-done = bf16[40,1024]{1,0:T(8,128)(2,1)S(1)} copy-done((bf16[40,1024]{1,0:T(8,128)(2,1)S(1)}, bf16[40,1024]{1,0:T(8,128)(2,1)}, u32[]{:S(2)}) %copy-start) | copy-done | bytes 81944
  0.9 0.7 copy-done.1
  1.6 0.3 shard_map.64
  1.9 6.2 %all_gather.3 = bf16[160,1024]{1,0:T(8,128)(2,1)S(1)} all-gather(bf16[40,1024]{1,0:T(8,128)(2,1)S(1)} %shard_map.64), channel_id=1, replica_groups={{0,32,64,96},{128,160,192,224},{256,288,320,352},{384,416,448,480},{1,3..., dimensions={0}, use_global_device_ids=true | all-gather | bytes 409600 | tf_op jit(solution)/shard_map/all_gather | solution.py:183
  8.1 15.2 %collective-permute-start = (bf16[160,1024]{1,0:T(8,128)(2,1)S(1)}, bf16[160,1024]{1,0:T(8,128)(2,1)S(1)}, u32[]{:S(2)}, u32[]{:S(2)}) collective-permute-start(bf16[160,1024]{1,0:T(8,128)(2,1)S(1)} %all_gather.3), channel_id=1, source_target_pairs={{0,6},{1,12},{2,47},{3,45},{4,81},{5,88},{6,115},{7,126},{8,130},{... | collective-permute-start | bytes 983048 | tf_op jit(solution)/shard_map/ppermute | solution.py:79
  23.4 1.2 %broadcast_in_dim.12 = bf16[4,160,1024]{2,1,0:T(8,128)(2,1)} broadcast(bf16[160,1024]{1,0:T(8,128)(2,1)S(1)} %all_gather.3), dimensions={1,2} | broadcast | bytes 1638400 | tf_op jit(solution)/shard_map/broadcast_in_dim | solution.py:188
  24.6 3.5 %all-to-all-start = ((bf16[4,160,1024]{2,1,0:T(8,128)(2,1)}), bf16[4,160,1024]{2,1,0:T(8,128)(2,1)S(1)}, u32[]{:S(2)}, u32[]{:S(2)}) async-start(bf16[4,160,1024]{2,1,0:T(8,128)(2,1)} %broadcast_in_dim.12), calls=%async_computation | async-start | bytes 2621440 | tf_op jit(solution)/shard_map/all_to_all | solution.py:187
  28.2 10.7 %collective-permute-done.refs_2_ = bf16[160,1024]{1,0:T(8,128)(2,1)S(1)} collective-permute-done((bf16[160,1024]{1,0:T(8,128)(2,1)S(1)}, bf16[160,1024]{1,0:T(8,128)(2,1)S(1)}, u32[]{:S(2)}, u32[]{:S(2)}) %collective-permute-start) | collective-permute-done | bytes 327712 | tf_op jit(solution)/shard_map/ppermute | solution.py:79
  38.8 4.2 %collective-permute-start.4 = (bf16[160,1024]{1,0:T(8,128)(2,1)S(1)}, bf16[160,1024]{1,0:T(8,128)(2,1)S(1)}, u32[]{:S(2)}, u32[]{:S(2)}) collective-permute-start(bf16[160,1024]{1,0:T(8,128)(2,1)S(1)} %collective-permute-done.refs_2_), channel_id=1, source_target_pairs={{0,15},{1,0},{2,1},{3,2},{4,3},{5,4},{6,5},{7,6},{8,7},{9,8},{10,9... | collective-permute-start | bytes 983048 | tf_op jit(solution)/shard_map/ppermute | solution.py:79
  43.0 1.9 %collective-permute-start.1 = (bf16[160,1024]{1,0:T(8,128)(2,1)S(1)}, bf16[160,1024]{1,0:T(8,128)(2,1)S(1)}, u32[]{:S(2)}, u32[]{:S(2)}) collective-permute-start(bf16[160,1024]{1,0:T(8,128)(2,1)S(1)} %collective-permute-done.refs_2_), channel_id=1, source_target_pairs={{0,1},{1,2},{2,3},{3,4},{4,5},{5,6},{6,7},{7,8},{8,9},{9,10},{10,1... | collective-permute-start | bytes 983048 | tf_op jit(solution)/shard_map/ppermute | solution.py:79
  44.9 0.0 copy-done.5
  45.0 0.0 copy-done.2
  45.0 0.6 gather_fusion
  45.6 9.5 %collective-permute-start.7 = (bf16[160,1024]{1,0:T(8,128)(2,1)S(1)}, bf16[160,1024]{1,0:T(8,128)(2,1)}, u32[]{:S(2)}, u32[]{:S(2)}) collective-permute-start(bf16[160,1024]{1,0:T(8,128)(2,1)S(1)} %collective-permute-done.refs_2_), channel_id=1, source_target_pairs={{0,16},{1,17},{2,18},{3,19},{4,20},{5,21},{6,22},{7,23},{8,24},{9,... | collective-permute-start | bytes 983048 | tf_op jit(solution)/shard_map/ppermute | solution.py:79
  55.1 0.0 collective-permute-done.4.refs_3_
  55.1 5.1 %collective-permute-start.5 = (bf16[160,1024]{1,0:T(8,128)(2,1)S(1)}, bf16[160,1024]{1,0:T(8,128)(2,1)S(1)}, u32[]{:S(2)}, u32[]{:S(2)}) collective-permute-start(bf16[160,1024]{1,0:T(8,128)(2,1)S(1)} %collective-permute-done.4.refs_3_), channel_id=1, source_target_pairs={{0,15},{1,0},{2,1},{3,2},{4,3},{5,4},{6,5},{7,6},{8,7},{9,8},{10,9... | collective-permute-start | bytes 983048 | tf_op jit(solution)/shard_map/ppermute | solution.py:79
  60.3 2.4 %collective-permute-start.6 = (bf16[160,1024]{1,0:T(8,128)(2,1)S(1)}, bf16[160,1024]{1,0:T(8,128)(2,1)S(1)}, u32[]{:S(2)}, u32[]{:S(2)}) collective-permute-start(bf16[160,1024]{1,0:T(8,128)(2,1)S(1)} %collective-permute-done.4.refs_3_), channel_id=1, source_target_pairs={{0,16},{1,17},{2,18},{3,19},{4,20},{5,21},{6,22},{7,23},{8,24},{9,... | collective-permute-start | bytes 983048 | tf_op jit(solution)/shard_map/ppermute | solution.py:79
  62.7 0.0 collective-permute-done.1.refs_2_
  62.7 1.9 %collective-permute-start.3 = (bf16[160,1024]{1,0:T(8,128)(2,1)S(1)}, bf16[160,1024]{1,0:T(8,128)(2,1)}, u32[]{:S(2)}, u32[]{:S(2)}) collective-permute-start(bf16[160,1024]{1,0:T(8,128)(2,1)S(1)} %collective-permute-done.1.refs_2_), channel_id=1, source_target_pairs={{0,1},{1,2},{2,3},{3,4},{4,5},{5,6},{6,7},{7,8},{8,9},{9,10},{10,1... | collective-permute-start | bytes 983048 | tf_op jit(solution)/shard_map/ppermute | solution.py:79
  64.6 5.0 %collective-permute-start.2 = (bf16[160,1024]{1,0:T(8,128)(2,1)S(1)}, bf16[160,1024]{1,0:T(8,128)(2,1)S(1)}, u32[]{:S(2)}, u32[]{:S(2)}) collective-permute-start(bf16[160,1024]{1,0:T(8,128)(2,1)S(1)} %collective-permute-done.1.refs_2_), channel_id=1, source_target_pairs={{0,16},{1,17},{2,18},{3,19},{4,20},{5,21},{6,22},{7,23},{8,24},{9,... | collective-permute-start | bytes 983048 | tf_op jit(solution)/shard_map/ppermute | solution.py:79
  69.6 0.0 all-to-all-done
  69.6 0.4 shard_map.65.refs_1_
  70.0 0.0 collective-permute-done.7.refs_4_
  70.0 2.7 %shard_map.66.refs_3_ = f32[8,160,640]{2,1,0:T(8,128)} custom-call(s32[8]{0:T(128)S(1)} %and_select_fusion.refs_0_, bf16[1024,640]{1,0:T(8,128)(2,1)S(1)} %shard_map.65.refs_1_, bf16[160,1024]{1,0:T(8,128)(2,1)S(1)} %collective-permute-done.refs_2_, bf16[160,1024]{1,0:T(8,128)(2,1)S(1)} %collective-permute-done.4.refs_3_, ...), custom_call_target="tpu_custom_call" | custom-call | flops 480 | bytes 480 | tf_op jit(solution)/shard_map/pallas_call | solution.py:161
  72.8 1.7 %shard_map.67.refs_4_ = f32[8,160,640]{2,1,0:T(8,128)} custom-call(s32[8]{0:T(128)S(1)} %and_select_fusion.refs_0_, bf16[1024,640]{1,0:T(8,128)(2,1)S(1)} %shard_map.65.refs_1_, bf16[160,1024]{1,0:T(8,128)(2,1)S(1)} %collective-permute-done.1.refs_2_, f32[8,160,640]{2,1,0:T(8,128)} %shard_map.66.refs_3_), custom_call_target="tpu_custom_call", output_to_operand_aliasing={{}: (3, {})} | custom-call | flops 160 | bytes 160 | tf_op jit(solution)/shard_map/pallas_call | solution.py:161
  74.5 0.0 collective-permute-done.5.refs_2_
  74.5 0.0 collective-permute-done.6.refs_3_
  74.6 2.0 %shard_map.68.refs_3_ = f32[8,160,640]{2,1,0:T(8,128)} custom-call(s32[8]{0:T(128)S(1)} %and_select_fusion.refs_0_, bf16[1024,640]{1,0:T(8,128)(2,1)S(1)} %shard_map.65.refs_1_, bf16[160,1024]{1,0:T(8,128)(2,1)S(1)} %collective-permute-done.5.refs_2_, bf16[160,1024]{1,0:T(8,128)(2,1)S(1)} %collective-permute-done.6.refs_3_, ...), custom_call_target="tpu_custom_call", output_to_operand_aliasing={{}: (4, {})} | custom-call | flops 320 | bytes 320 | tf_op jit(solution)/shard_map/pallas_call | solution.py:161
  76.6 0.0 collective-permute-done.3.refs_2_
  76.6 2.2 %shard_map.69.refs_3_ = f32[8,160,640]{2,1,0:T(8,128)} custom-call(s32[8]{0:T(128)S(1)} %and_select_fusion.refs_0_, bf16[1024,640]{1,0:T(8,128)(2,1)S(1)} %shard_map.65.refs_1_, bf16[160,1024]{1,0:T(8,128)(2,1)} %collective-permute-done.3.refs_2_, f32[8,160,640]{2,1,0:T(8,128)} %shard_map.68.refs_3_), custom_call_target="tpu_custom_call", output_to_operand_aliasing={{}: (3, {})} | custom-call | flops 160 | bytes 160 | tf_op jit(solution)/shard_map/pallas_call | solution.py:161
  78.8 0.0 collective-permute-done.2.refs_2_
  78.8 1.7 %shard_map.70 = f32[8,160,640]{2,1,0:T(8,128)} custom-call(s32[8]{0:T(128)S(1)} %and_select_fusion.refs_0_, bf16[1024,640]{1,0:T(8,128)(2,1)S(1)} %shard_map.65.refs_1_, bf16[160,1024]{1,0:T(8,128)(2,1)S(1)} %collective-permute-done.2.refs_2_, f32[8,160,640]{2,1,0:T(8,128)} %shard_map.69.refs_3_), custom_call_target="tpu_custom_call", output_to_operand_aliasing={{}: (3, {})} | custom-call | flops 160 | bytes 160 | tf_op jit(solution)/shard_map/pallas_call | solution.py:161
  (12 shorter events, 0.1 us)
Async XLA Ops:
  0.0 44.9 %copy-start.5 = (s32[8]{0:T(128)S(1)}, s32[8]{0:T(128)}, u32[]{:S(2)}) copy-start(s32[8]{0:T(128)} %constant.82.clone) | copy-start | bytes 100
  0.0 45.0 %copy-start.2 = (s32[128]{0:T(128)S(1)}, s32[128]{0:T(128)}, u32[]{:S(2)}) copy-start(s32[128]{0:T(128)} %constant.86) | copy-start | bytes 1540
  0.0 0.9 %copy-start = (bf16[40,1024]{1,0:T(8,128)(2,1)S(1)}, bf16[40,1024]{1,0:T(8,128)(2,1)}, u32[]{:S(2)}) copy-start(bf16[40,1024]{1,0:T(8,128)(2,1)} %mantissa_ref.1) | copy-start | bytes 245764
  0.9 0.7 copy-start.1
  1.6 68.0 %copy-start.3 = (s32[1024]{0:T(1024)S(1)}, s32[1024]{0:T(1024)}, u32[]{:S(2)}) copy-start(s32[1024]{0:T(1024)} %param.9) | copy-start | bytes 12292
  1.6 68.0 %copy-start.4 = (s32[1024]{0:T(1024)S(1)}, s32[1024]{0:T(1024)}, u32[]{:S(2)}) copy-start(s32[1024]{0:T(1024)} %param.8) | copy-start | bytes 12292
  8.1 30.7 %collective-permute-start = (bf16[160,1024]{1,0:T(8,128)(2,1)S(1)}, bf16[160,1024]{1,0:T(8,128)(2,1)S(1)}, u32[]{:S(2)}, u32[]{:S(2)}) collective-permute-start(bf16[160,1024]{1,0:T(8,128)(2,1)S(1)} %all_gather.3), channel_id=1, source_target_pairs={{0,6},{1,12},{2,47},{3,45},{4,81},{5,88},{6,115},{7,126},{8,130},{... | collective-permute-start | bytes 983048 | tf_op jit(solution)/shard_map/ppermute | solution.py:79
  24.6 45.0 %all-to-all-start = ((bf16[4,160,1024]{2,1,0:T(8,128)(2,1)}), bf16[4,160,1024]{2,1,0:T(8,128)(2,1)S(1)}, u32[]{:S(2)}, u32[]{:S(2)}) async-start(bf16[4,160,1024]{2,1,0:T(8,128)(2,1)} %broadcast_in_dim.12), calls=%async_computation | async-start | bytes 2621440 | tf_op jit(solution)/shard_map/all_to_all | solution.py:187
  38.8 16.3 %collective-permute-start.4 = (bf16[160,1024]{1,0:T(8,128)(2,1)S(1)}, bf16[160,1024]{1,0:T(8,128)(2,1)S(1)}, u32[]{:S(2)}, u32[]{:S(2)}) collective-permute-start(bf16[160,1024]{1,0:T(8,128)(2,1)S(1)} %collective-permute-done.refs_2_), channel_id=1, source_target_pairs={{0,15},{1,0},{2,1},{3,2},{4,3},{5,4},{6,5},{7,6},{8,7},{9,8},{10,9... | collective-permute-start | bytes 983048 | tf_op jit(solution)/shard_map/ppermute | solution.py:79
  43.0 19.7 %collective-permute-start.1 = (bf16[160,1024]{1,0:T(8,128)(2,1)S(1)}, bf16[160,1024]{1,0:T(8,128)(2,1)S(1)}, u32[]{:S(2)}, u32[]{:S(2)}) collective-permute-start(bf16[160,1024]{1,0:T(8,128)(2,1)S(1)} %collective-permute-done.refs_2_), channel_id=1, source_target_pairs={{0,1},{1,2},{2,3},{3,4},{4,5},{5,6},{6,7},{7,8},{8,9},{9,10},{10,1... | collective-permute-start | bytes 983048 | tf_op jit(solution)/shard_map/ppermute | solution.py:79
  45.6 24.4 %collective-permute-start.7 = (bf16[160,1024]{1,0:T(8,128)(2,1)S(1)}, bf16[160,1024]{1,0:T(8,128)(2,1)}, u32[]{:S(2)}, u32[]{:S(2)}) collective-permute-start(bf16[160,1024]{1,0:T(8,128)(2,1)S(1)} %collective-permute-done.refs_2_), channel_id=1, source_target_pairs={{0,16},{1,17},{2,18},{3,19},{4,20},{5,21},{6,22},{7,23},{8,24},{9,... | collective-permute-start | bytes 983048 | tf_op jit(solution)/shard_map/ppermute | solution.py:79
  55.1 19.4 %collective-permute-start.5 = (bf16[160,1024]{1,0:T(8,128)(2,1)S(1)}, bf16[160,1024]{1,0:T(8,128)(2,1)S(1)}, u32[]{:S(2)}, u32[]{:S(2)}) collective-permute-start(bf16[160,1024]{1,0:T(8,128)(2,1)S(1)} %collective-permute-done.4.refs_3_), channel_id=1, source_target_pairs={{0,15},{1,0},{2,1},{3,2},{4,3},{5,4},{6,5},{7,6},{8,7},{9,8},{10,9... | collective-permute-start | bytes 983048 | tf_op jit(solution)/shard_map/ppermute | solution.py:79
  60.3 14.3 %collective-permute-start.6 = (bf16[160,1024]{1,0:T(8,128)(2,1)S(1)}, bf16[160,1024]{1,0:T(8,128)(2,1)S(1)}, u32[]{:S(2)}, u32[]{:S(2)}) collective-permute-start(bf16[160,1024]{1,0:T(8,128)(2,1)S(1)} %collective-permute-done.4.refs_3_), channel_id=1, source_target_pairs={{0,16},{1,17},{2,18},{3,19},{4,20},{5,21},{6,22},{7,23},{8,24},{9,... | collective-permute-start | bytes 983048 | tf_op jit(solution)/shard_map/ppermute | solution.py:79
  62.7 13.9 %collective-permute-start.3 = (bf16[160,1024]{1,0:T(8,128)(2,1)S(1)}, bf16[160,1024]{1,0:T(8,128)(2,1)}, u32[]{:S(2)}, u32[]{:S(2)}) collective-permute-start(bf16[160,1024]{1,0:T(8,128)(2,1)S(1)} %collective-permute-done.1.refs_2_), channel_id=1, source_target_pairs={{0,1},{1,2},{2,3},{3,4},{4,5},{5,6},{6,7},{7,8},{8,9},{9,10},{10,1... | collective-permute-start | bytes 983048 | tf_op jit(solution)/shard_map/ppermute | solution.py:79
  64.6 14.2 %collective-permute-start.2 = (bf16[160,1024]{1,0:T(8,128)(2,1)S(1)}, bf16[160,1024]{1,0:T(8,128)(2,1)S(1)}, u32[]{:S(2)}, u32[]{:S(2)}) collective-permute-start(bf16[160,1024]{1,0:T(8,128)(2,1)S(1)} %collective-permute-done.1.refs_2_), channel_id=1, source_target_pairs={{0,16},{1,17},{2,18},{3,19},{4,20},{5,21},{6,22},{7,23},{8,24},{9,... | collective-permute-start | bytes 983048 | tf_op jit(solution)/shard_map/ppermute | solution.py:79

commit v7 on v6

--- a/solution.py
+++ b/solution.py
@@ -79,31 +79,20 @@
     return lax.ppermute(block, JOINT, pairs)
 
 
-def dequantize_body(mantissa_ref, exponent_ref, out, mantissa, exponent, sems):
-    first = pltpu.make_async_copy(mantissa_ref, mantissa, sems.at[0])
-    second = pltpu.make_async_copy(exponent_ref, exponent, sems.at[1])
-    first.start()
-    second.start()
-    second.wait()
+def dequantize_body(mantissa, exponent, out):
     scale = jnp.exp2(exponent[...].astype(jnp.float32)).T
-    first.wait()
     for k in range(DEPTH // 128):
         span = slice(128 * k, 128 * (k + 1))
         out[:, span] = (mantissa[:, span].astype(jnp.float32) * scale[:, k : k + 1]).astype(jnp.bfloat16)
 
 
 def dequantize(mantissa, exponent):
-    anywhere = pl.BlockSpec(memory_space=pltpu.HBM)
+    whole = pl.BlockSpec(memory_space=pltpu.VMEM)
     return pl.pallas_call(
         dequantize_body,
         out_shape=jax.ShapeDtypeStruct(mantissa.shape, jnp.bfloat16),
-        in_specs=[anywhere, anywhere],
-        out_specs=pl.BlockSpec(memory_space=pltpu.VMEM),
-        scratch_shapes=[
-            pltpu.VMEM(mantissa.shape, mantissa.dtype),
-            pltpu.VMEM(exponent.shape[::-1], exponent.dtype),
-            pltpu.SemaphoreType.DMA((2,)),
-        ],
+        in_specs=[whole, whole],
+        out_specs=whole,
         compiler_params=pltpu.CompilerParams(vmem_limit_bytes=LIMIT),
     )(mantissa, exponent.T)
 

time: 81.1 us -> 81 us (level)
  no operation moved by 1% of the time
where the time goes in v7:
time: 81 us; the launch traced here: 80.4 us
  starting transfers between devices  48.7 us (60%)
  Pallas kernels  11 us (14%)
  waiting for transfers between devices  10.7 us (13%)
  blocking collectives  6.19 us (8%)
  local copies, waits for them, and re-layouts  3.48 us (4%)
    ppermute x8, starting transfers between devices, send(): return lax.ppermute(block, JOINT, pairs)  45.2 us
    ppermute x8, waiting for transfers between devices, send(): return lax.ppermute(block, JOINT, pairs)  10.7 us
    pallas_call x5, Pallas kernels, multiply(): pl.pallas_call(body, out_shape=jax.ShapeDtypeStruct((CHUNKS, ROWS, COLS),...  10.4 us
    all_gather x1, blocking collectives, per_device(): lax.all_gather(own, 'prow', axis=0, tiled=True, axis_index_groups=same_x)  6.19 us
    all_to_all x1, starting transfers between devices, per_device(): lax.all_to_all(jnp.broadcast_to(group, (NX, *group.shape)), 'prow', 0, 0,...  3.53 us
  transfers between devices with their start and end apart: 9, of which 1 were waited for; matrix products, arithmetic and copies ran while one was open for 2% of the time, Pallas kernels for 11%

profile of v7, /device:TPU:2, one launch (start us, length us, event | category | flops | bytes accessed | tf_op | source)
XLA Modules:
  0.0 80.4 jit_solution(16794328494669721079)
XLA Ops:
  0.0 0.9 %copy-done = bf16[40,1024]{1,0:T(8,128)(2,1)S(1)} copy-done((bf16[40,1024]{1,0:T(8,128)(2,1)S(1)}, bf16[40,1024]{1,0:T(8,128)(2,1)}, u32[]{:S(2)}) %copy-start) | copy-done | bytes 81944
  0.9 0.7 copy-done.1
  1.6 0.2 shard_map.64
  1.8 6.2 %all_gather.3 = bf16[160,1024]{1,0:T(8,128)(2,1)S(1)} all-gather(bf16[40,1024]{1,0:T(8,128)(2,1)S(1)} %shard_map.64), channel_id=1, replica_groups={{0,32,64,96},{128,160,192,224},{256,288,320,352},{384,416,448,480},{1,3..., dimensions={0}, use_global_device_ids=true | all-gather | bytes 409600 | tf_op jit(solution)/shard_map/all_gather | solution.py:172
  8.0 15.2 %collective-permute-start = (bf16[160,1024]{1,0:T(8,128)(2,1)S(1)}, bf16[160,1024]{1,0:T(8,128)(2,1)S(1)}, u32[]{:S(2)}, u32[]{:S(2)}) collective-permute-start(bf16[160,1024]{1,0:T(8,128)(2,1)S(1)} %all_gather.3), channel_id=1, source_target_pairs={{0,6},{1,12},{2,47},{3,45},{4,81},{5,88},{6,115},{7,126},{8,130},{... | collective-permute-start | bytes 983048 | tf_op jit(solution)/shard_map/ppermute | solution.py:79
  23.3 1.2 %broadcast_in_dim.12 = bf16[4,160,1024]{2,1,0:T(8,128)(2,1)} broadcast(bf16[160,1024]{1,0:T(8,128)(2,1)S(1)} %all_gather.3), dimensions={1,2} | broadcast | bytes 1638400 | tf_op jit(solution)/shard_map/broadcast_in_dim | solution.py:177
  24.5 3.5 %all-to-all-start = ((bf16[4,160,1024]{2,1,0:T(8,128)(2,1)}), bf16[4,160,1024]{2,1,0:T(8,128)(2,1)S(1)}, u32[]{:S(2)}, u32[]{:S(2)}) async-start(bf16[4,160,1024]{2,1,0:T(8,128)(2,1)} %broadcast_in_dim.12), calls=%async_computation | async-start | bytes 2621440 | tf_op jit(solution)/shard_map/all_to_all | solution.py:176
  28.1 10.7 %collective-permute-done.refs_2_ = bf16[160,1024]{1,0:T(8,128)(2,1)S(1)} collective-permute-done((bf16[160,1024]{1,0:T(8,128)(2,1)S(1)}, bf16[160,1024]{1,0:T(8,128)(2,1)S(1)}, u32[]{:S(2)}, u32[]{:S(2)}) %collective-permute-start) | collective-permute-done | bytes 327712 | tf_op jit(solution)/shard_map/ppermute | solution.py:79
  38.7 4.2 %collective-permute-start.4 = (bf16[160,1024]{1,0:T(8,128)(2,1)S(1)}, bf16[160,1024]{1,0:T(8,128)(2,1)S(1)}, u32[]{:S(2)}, u32[]{:S(2)}) collective-permute-start(bf16[160,1024]{1,0:T(8,128)(2,1)S(1)} %collective-permute-done.refs_2_), channel_id=1, source_target_pairs={{0,15},{1,0},{2,1},{3,2},{4,3},{5,4},{6,5},{7,6},{8,7},{9,8},{10,9... | collective-permute-start | bytes 983048 | tf_op jit(solution)/shard_map/ppermute | solution.py:79
  42.9 1.9 %collective-permute-start.1 = (bf16[160,1024]{1,0:T(8,128)(2,1)S(1)}, bf16[160,1024]{1,0:T(8,128)(2,1)S(1)}, u32[]{:S(2)}, u32[]{:S(2)}) collective-permute-start(bf16[160,1024]{1,0:T(8,128)(2,1)S(1)} %collective-permute-done.refs_2_), channel_id=1, source_target_pairs={{0,1},{1,2},{2,3},{3,4},{4,5},{5,6},{6,7},{7,8},{8,9},{9,10},{10,1... | collective-permute-start | bytes 983048 | tf_op jit(solution)/shard_map/ppermute | solution.py:79
  44.8 0.0 copy-done.5
  44.9 0.0 copy-done.2
  44.9 0.6 gather_fusion
  45.5 9.5 %collective-permute-start.7 = (bf16[160,1024]{1,0:T(8,128)(2,1)S(1)}, bf16[160,1024]{1,0:T(8,128)(2,1)}, u32[]{:S(2)}, u32[]{:S(2)}) collective-permute-start(bf16[160,1024]{1,0:T(8,128)(2,1)S(1)} %collective-permute-done.refs_2_), channel_id=1, source_target_pairs={{0,16},{1,17},{2,18},{3,19},{4,20},{5,21},{6,22},{7,23},{8,24},{9,... | collective-permute-start | bytes 983048 | tf_op jit(solution)/shard_map/ppermute | solution.py:79
  55.0 0.0 collective-permute-done.4.refs_3_
  55.0 5.1 %collective-permute-start.5 = (bf16[160,1024]{1,0:T(8,128)(2,1)S(1)}, bf16[160,1024]{1,0:T(8,128)(2,1)S(1)}, u32[]{:S(2)}, u32[]{:S(2)}) collective-permute-start(bf16[160,1024]{1,0:T(8,128)(2,1)S(1)} %collective-permute-done.4.refs_3_), channel_id=1, source_target_pairs={{0,15},{1,0},{2,1},{3,2},{4,3},{5,4},{6,5},{7,6},{8,7},{9,8},{10,9... | collective-permute-start | bytes 983048 | tf_op jit(solution)/shard_map/ppermute | solution.py:79
  60.2 2.4 %collective-permute-start.6 = (bf16[160,1024]{1,0:T(8,128)(2,1)S(1)}, bf16[160,1024]{1,0:T(8,128)(2,1)S(1)}, u32[]{:S(2)}, u32[]{:S(2)}) collective-permute-start(bf16[160,1024]{1,0:T(8,128)(2,1)S(1)} %collective-permute-done.4.refs_3_), channel_id=1, source_target_pairs={{0,16},{1,17},{2,18},{3,19},{4,20},{5,21},{6,22},{7,23},{8,24},{9,... | collective-permute-start | bytes 983048 | tf_op jit(solution)/shard_map/ppermute | solution.py:79
  62.6 0.0 collective-permute-done.1.refs_2_
  62.6 1.9 %collective-permute-start.3 = (bf16[160,1024]{1,0:T(8,128)(2,1)S(1)}, bf16[160,1024]{1,0:T(8,128)(2,1)}, u32[]{:S(2)}, u32[]{:S(2)}) collective-permute-start(bf16[160,1024]{1,0:T(8,128)(2,1)S(1)} %collective-permute-done.1.refs_2_), channel_id=1, source_target_pairs={{0,1},{1,2},{2,3},{3,4},{4,5},{5,6},{6,7},{7,8},{8,9},{9,10},{10,1... | collective-permute-start | bytes 983048 | tf_op jit(solution)/shard_map/ppermute | solution.py:79
  64.5 5.0 %collective-permute-start.2 = (bf16[160,1024]{1,0:T(8,128)(2,1)S(1)}, bf16[160,1024]{1,0:T(8,128)(2,1)S(1)}, u32[]{:S(2)}, u32[]{:S(2)}) collective-permute-start(bf16[160,1024]{1,0:T(8,128)(2,1)S(1)} %collective-permute-done.1.refs_2_), channel_id=1, source_target_pairs={{0,16},{1,17},{2,18},{3,19},{4,20},{5,21},{6,22},{7,23},{8,24},{9,... | collective-permute-start | bytes 983048 | tf_op jit(solution)/shard_map/ppermute | solution.py:79
  69.5 0.0 all-to-all-done
  69.5 0.4 shard_map.65.refs_1_
  69.9 0.0 collective-permute-done.7.refs_4_
  69.9 2.7 %shard_map.66.refs_3_ = f32[8,160,640]{2,1,0:T(8,128)} custom-call(s32[8]{0:T(128)S(1)} %and_select_fusion.refs_0_, bf16[1024,640]{1,0:T(8,128)(2,1)S(1)} %shard_map.65.refs_1_, bf16[160,1024]{1,0:T(8,128)(2,1)S(1)} %collective-permute-done.refs_2_, bf16[160,1024]{1,0:T(8,128)(2,1)S(1)} %collective-permute-done.4.refs_3_, ...), custom_call_target="tpu_custom_call" | custom-call | flops 480 | bytes 480 | tf_op jit(solution)/shard_map/pallas_call | solution.py:150
  72.7 1.7 %shard_map.67.refs_4_ = f32[8,160,640]{2,1,0:T(8,128)} custom-call(s32[8]{0:T(128)S(1)} %and_select_fusion.refs_0_, bf16[1024,640]{1,0:T(8,128)(2,1)S(1)} %shard_map.65.refs_1_, bf16[160,1024]{1,0:T(8,128)(2,1)S(1)} %collective-permute-done.1.refs_2_, f32[8,160,640]{2,1,0:T(8,128)} %shard_map.66.refs_3_), custom_call_target="tpu_custom_call", output_to_operand_aliasing={{}: (3, {})} | custom-call | flops 160 | bytes 160 | tf_op jit(solution)/shard_map/pallas_call | solution.py:150
  74.4 0.0 collective-permute-done.5.refs_2_
  74.4 0.0 collective-permute-done.6.refs_3_
  74.5 2.0 %shard_map.68.refs_3_ = f32[8,160,640]{2,1,0:T(8,128)} custom-call(s32[8]{0:T(128)S(1)} %and_select_fusion.refs_0_, bf16[1024,640]{1,0:T(8,128)(2,1)S(1)} %shard_map.65.refs_1_, bf16[160,1024]{1,0:T(8,128)(2,1)S(1)} %collective-permute-done.5.refs_2_, bf16[160,1024]{1,0:T(8,128)(2,1)S(1)} %collective-permute-done.6.refs_3_, ...), custom_call_target="tpu_custom_call", output_to_operand_aliasing={{}: (4, {})} | custom-call | flops 320 | bytes 320 | tf_op jit(solution)/shard_map/pallas_call | solution.py:150
  76.5 0.0 collective-permute-done.3.refs_2_
  76.5 2.2 %shard_map.69.refs_3_ = f32[8,160,640]{2,1,0:T(8,128)} custom-call(s32[8]{0:T(128)S(1)} %and_select_fusion.refs_0_, bf16[1024,640]{1,0:T(8,128)(2,1)S(1)} %shard_map.65.refs_1_, bf16[160,1024]{1,0:T(8,128)(2,1)} %collective-permute-done.3.refs_2_, f32[8,160,640]{2,1,0:T(8,128)} %shard_map.68.refs_3_), custom_call_target="tpu_custom_call", output_to_operand_aliasing={{}: (3, {})} | custom-call | flops 160 | bytes 160 | tf_op jit(solution)/shard_map/pallas_call | solution.py:150
  78.7 0.0 collective-permute-done.2.refs_2_
  78.7 1.7 %shard_map.70 = f32[8,160,640]{2,1,0:T(8,128)} custom-call(s32[8]{0:T(128)S(1)} %and_select_fusion.refs_0_, bf16[1024,640]{1,0:T(8,128)(2,1)S(1)} %shard_map.65.refs_1_, bf16[160,1024]{1,0:T(8,128)(2,1)S(1)} %collective-permute-done.2.refs_2_, f32[8,160,640]{2,1,0:T(8,128)} %shard_map.69.refs_3_), custom_call_target="tpu_custom_call", output_to_operand_aliasing={{}: (3, {})} | custom-call | flops 160 | bytes 160 | tf_op jit(solution)/shard_map/pallas_call | solution.py:150
  (12 shorter events, 0.1 us)
Async XLA Ops:
  0.0 44.8 %copy-start.5 = (s32[8]{0:T(128)S(1)}, s32[8]{0:T(128)}, u32[]{:S(2)}) copy-start(s32[8]{0:T(128)} %constant.82.clone) | copy-start | bytes 100
  0.0 44.9 %copy-start.2 = (s32[128]{0:T(128)S(1)}, s32[128]{0:T(128)}, u32[]{:S(2)}) copy-start(s32[128]{0:T(128)} %constant.86) | copy-start | bytes 1540
  0.0 0.9 %copy-start = (bf16[40,1024]{1,0:T(8,128)(2,1)S(1)}, bf16[40,1024]{1,0:T(8,128)(2,1)}, u32[]{:S(2)}) copy-start(bf16[40,1024]{1,0:T(8,128)(2,1)} %mantissa.1) | copy-start | bytes 245764
  0.9 0.7 copy-start.1
  1.6 67.9 %copy-start.3 = (s32[1024]{0:T(1024)S(1)}, s32[1024]{0:T(1024)}, u32[]{:S(2)}) copy-start(s32[1024]{0:T(1024)} %param.9) | copy-start | bytes 12292
  1.6 67.9 %copy-start.4 = (s32[1024]{0:T(1024)S(1)}, s32[1024]{0:T(1024)}, u32[]{:S(2)}) copy-start(s32[1024]{0:T(1024)} %param.8) | copy-start | bytes 12292
  8.0 30.7 %collective-permute-start = (bf16[160,1024]{1,0:T(8,128)(2,1)S(1)}, bf16[160,1024]{1,0:T(8,128)(2,1)S(1)}, u32[]{:S(2)}, u32[]{:S(2)}) collective-permute-start(bf16[160,1024]{1,0:T(8,128)(2,1)S(1)} %all_gather.3), channel_id=1, source_target_pairs={{0,6},{1,12},{2,47},{3,45},{4,81},{5,88},{6,115},{7,126},{8,130},{... | collective-permute-start | bytes 983048 | tf_op jit(solution)/shard_map/ppermute | solution.py:79
  24.5 45.0 %all-to-all-start = ((bf16[4,160,1024]{2,1,0:T(8,128)(2,1)}), bf16[4,160,1024]{2,1,0:T(8,128)(2,1)S(1)}, u32[]{:S(2)}, u32[]{:S(2)}) async-start(bf16[4,160,1024]{2,1,0:T(8,128)(2,1)} %broadcast_in_dim.12), calls=%async_computation | async-start | bytes 2621440 | tf_op jit(solution)/shard_map/all_to_all | solution.py:176
  38.7 16.3 %collective-permute-start.4 = (bf16[160,1024]{1,0:T(8,128)(2,1)S(1)}, bf16[160,1024]{1,0:T(8,128)(2,1)S(1)}, u32[]{:S(2)}, u32[]{:S(2)}) collective-permute-start(bf16[160,1024]{1,0:T(8,128)(2,1)S(1)} %collective-permute-done.refs_2_), channel_id=1, source_target_pairs={{0,15},{1,0},{2,1},{3,2},{4,3},{5,4},{6,5},{7,6},{8,7},{9,8},{10,9... | collective-permute-start | bytes 983048 | tf_op jit(solution)/shard_map/ppermute | solution.py:79
  42.9 19.7 %collective-permute-start.1 = (bf16[160,1024]{1,0:T(8,128)(2,1)S(1)}, bf16[160,1024]{1,0:T(8,128)(2,1)S(1)}, u32[]{:S(2)}, u32[]{:S(2)}) collective-permute-start(bf16[160,1024]{1,0:T(8,128)(2,1)S(1)} %collective-permute-done.refs_2_), channel_id=1, source_target_pairs={{0,1},{1,2},{2,3},{3,4},{4,5},{5,6},{6,7},{7,8},{8,9},{9,10},{10,1... | collective-permute-start | bytes 983048 | tf_op jit(solution)/shard_map/ppermute | solution.py:79
  45.5 24.4 %collective-permute-start.7 = (bf16[160,1024]{1,0:T(8,128)(2,1)S(1)}, bf16[160,1024]{1,0:T(8,128)(2,1)}, u32[]{:S(2)}, u32[]{:S(2)}) collective-permute-start(bf16[160,1024]{1,0:T(8,128)(2,1)S(1)} %collective-permute-done.refs_2_), channel_id=1, source_target_pairs={{0,16},{1,17},{2,18},{3,19},{4,20},{5,21},{6,22},{7,23},{8,24},{9,... | collective-permute-start | bytes 983048 | tf_op jit(solution)/shard_map/ppermute | solution.py:79
  55.0 19.4 %collective-permute-start.5 = (bf16[160,1024]{1,0:T(8,128)(2,1)S(1)}, bf16[160,1024]{1,0:T(8,128)(2,1)S(1)}, u32[]{:S(2)}, u32[]{:S(2)}) collective-permute-start(bf16[160,1024]{1,0:T(8,128)(2,1)S(1)} %collective-permute-done.4.refs_3_), channel_id=1, source_target_pairs={{0,15},{1,0},{2,1},{3,2},{4,3},{5,4},{6,5},{7,6},{8,7},{9,8},{10,9... | collective-permute-start | bytes 983048 | tf_op jit(solution)/shard_map/ppermute | solution.py:79
  60.2 14.3 %collective-permute-start.6 = (bf16[160,1024]{1,0:T(8,128)(2,1)S(1)}, bf16[160,1024]{1,0:T(8,128)(2,1)S(1)}, u32[]{:S(2)}, u32[]{:S(2)}) collective-permute-start(bf16[160,1024]{1,0:T(8,128)(2,1)S(1)} %collective-permute-done.4.refs_3_), channel_id=1, source_target_pairs={{0,16},{1,17},{2,18},{3,19},{4,20},{5,21},{6,22},{7,23},{8,24},{9,... | collective-permute-start | bytes 983048 | tf_op jit(solution)/shard_map/ppermute | solution.py:79
  62.6 13.9 %collective-permute-start.3 = (bf16[160,1024]{1,0:T(8,128)(2,1)S(1)}, bf16[160,1024]{1,0:T(8,128)(2,1)}, u32[]{:S(2)}, u32[]{:S(2)}) collective-permute-start(bf16[160,1024]{1,0:T(8,128)(2,1)S(1)} %collective-permute-done.1.refs_2_), channel_id=1, source_target_pairs={{0,1},{1,2},{2,3},{3,4},{4,5},{5,6},{6,7},{7,8},{8,9},{9,10},{10,1... | collective-permute-start | bytes 983048 | tf_op jit(solution)/shard_map/ppermute | solution.py:79
  64.5 14.2 %collective-permute-start.2 = (bf16[160,1024]{1,0:T(8,128)(2,1)S(1)}, bf16[160,1024]{1,0:T(8,128)(2,1)S(1)}, u32[]{:S(2)}, u32[]{:S(2)}) collective-permute-start(bf16[160,1024]{1,0:T(8,128)(2,1)S(1)} %collective-permute-done.1.refs_2_), channel_id=1, source_target_pairs={{0,16},{1,17},{2,18},{3,19},{4,20},{5,21},{6,22},{7,23},{8,24},{9,... | collective-permute-start | bytes 983048 | tf_op jit(solution)/shard_map/ppermute | solution.py:79
